TPU v7x, 128 devices: a whole 4x4x4 slice. The times are simulated.
128 devices in a mesh: row: 4 (over z), col: 32 (over x, y, core).
Axes of the slice: x: 4, y: 4, z: 4, core: 2. Of those that a mesh axis runs over, the one named last changes fastest.
Arguments:
- tokens: bfloat16 [32768, 1024], P(('row', 'col')), may hold values from -6 to 6
- out_grad: bfloat16 [32768, 1024], P(('row', 'col')), may hold values from -6 to 6
- expert_ids: int32 [32768], P(('row', 'col')), may hold values from 0 to 127, as said below
- router_logits: float32 [32768, 128], P(('row', 'col')), may hold values from -6 to 273
- router_weight: bfloat16 [128, 1024], P(('row', 'col')), may hold values from -0.1875 to 0.1875
- w_in: bfloat16 [128, 1024, 2048], P(('row', 'col')), may hold values from -0.1875 to 0.1875
- w_out: bfloat16 [128, 2048, 1024], P(('row', 'col')), may hold values from -0.125 to 0.125
Outputs:
- d_tokens: bfloat16 [32768, 1024], P(('row', 'col'))
- d_w_in: bfloat16 [128, 1024, 2048], P(('row', 'col'))
- d_w_out: bfloat16 [128, 2048, 1024], P(('row', 'col'))
- d_router: float32 [128, 1024], P(('row', 'col'))
Inputs may be any that keep to these rules, and one draw needn't show every extreme that they name: `expert_ids`: among the 256 tokens of one device no expert is chosen more than 4 times, and one expert is chosen exactly 4 times by the tokens of every device.
All inputs are finite; a program needn't handle non-finite values.
Results may differ from a plain program's by a relative error of at most 0.017.
Values may be sent and summed in bfloat16 or wider, within the bound.
No kernel may reach another device: no remote copies, remote signals or barrier semaphores. Data moves between devices by JAX's collectives and lax.ppermute only.
A program may use at most 128 MiB of HBM per device.

v0:
```python
import jax
import jax.numpy as jnp
from jax import lax
from jax.sharding import PartitionSpec as P


def slot_layout(expert_ids, experts, capacity):
    onehot = (expert_ids[:, None] == jnp.arange(experts, dtype=jnp.int32)[None, :]).astype(
        jnp.int32
    )
    earlier = jnp.cumsum(onehot, axis=0) - onehot
    ranks = jnp.sum(earlier * onehot, axis=1)
    return (onehot, expert_ids * capacity + ranks)


def expert_pass(routed, scaled_rows, inner_weight, outer_weight):
    pre_act = jnp.dot(routed, inner_weight, preferred_element_type=jnp.float32)
    hidden = jnp.maximum(pre_act, 0.0).astype(jnp.bfloat16)
    expert_out = jnp.dot(hidden, outer_weight, preferred_element_type=jnp.float32).astype(
        jnp.bfloat16
    )
    back = jnp.dot(scaled_rows, outer_weight.T, preferred_element_type=jnp.float32)
    hidden_grad = jnp.where(pre_act > 0.0, back, 0.0).astype(jnp.bfloat16)
    grad_in = jnp.dot(hidden_grad, inner_weight.T, preferred_element_type=jnp.float32).astype(
        jnp.bfloat16
    )
    return (hidden, hidden_grad, expert_out, grad_in)


def weight_grads(routed, scaled_rows, hidden, hidden_grad):
    grad_inner = jnp.dot(routed.T, hidden_grad, preferred_element_type=jnp.float32).astype(
        jnp.bfloat16
    )
    grad_outer = jnp.dot(hidden.T, scaled_rows, preferred_element_type=jnp.float32).astype(
        jnp.bfloat16
    )
    return (grad_inner, grad_outer)


def per_device(tokens, out_grad, expert_ids, router_logits, router_weight, w_in, w_out):
    n_row = lax.axis_size("row")
    n_col = lax.axis_size("col")
    experts = n_row * n_col
    tok_count, width = tokens.shape
    capacity = max(2, 2 * tok_count // experts)
    slots = experts * capacity
    onehot, slot = slot_layout(expert_ids, experts, capacity)
    chosen = onehot.astype(jnp.float32)
    probs = jax.nn.softmax(router_logits, axis=-1)
    gate = jnp.sum(probs * chosen, axis=1)
    send_rows = jnp.zeros((slots, width), jnp.bfloat16).at[slot].set(tokens)
    scaled = (gate[:, None] * out_grad.astype(jnp.float32)).astype(jnp.bfloat16)
    send_second = jnp.zeros((slots, width), jnp.bfloat16).at[slot].set(scaled)
    routed, second_rows = (
        lax.all_to_all(
            lax.all_to_all(
                send_rows.reshape(n_row, n_col, capacity, width),
                "row",
                split_axis=0,
                concat_axis=0,
                tiled=True,
            ),
            "col",
            split_axis=1,
            concat_axis=1,
            tiled=True,
        ),
        lax.all_to_all(
            lax.all_to_all(
                send_second.reshape(n_row, n_col, capacity, width),
                "row",
                split_axis=0,
                concat_axis=0,
                tiled=True,
            ),
            "col",
            split_axis=1,
            concat_axis=1,
            tiled=True,
        ),
    )
    routed = routed.reshape(slots, width)
    second_rows = second_rows.reshape(slots, width)
    inner_weight = w_in[0]
    outer_weight = w_out[0]
    hidden, hidden_grad, expert_out, grad_in = expert_pass(
        routed, second_rows, inner_weight, outer_weight
    )
    grad_inner, grad_outer = weight_grads(routed, second_rows, hidden, hidden_grad)
    back_in, back_out = (
        lax.all_to_all(
            lax.all_to_all(
                grad_in.reshape(n_row, n_col, capacity, width),
                "row",
                split_axis=0,
                concat_axis=0,
                tiled=True,
            ),
            "col",
            split_axis=1,
            concat_axis=1,
            tiled=True,
        ),
        lax.all_to_all(
            lax.all_to_all(
                expert_out.reshape(n_row, n_col, capacity, width),
                "row",
                split_axis=0,
                concat_axis=0,
                tiled=True,
            ),
            "col",
            split_axis=1,
            concat_axis=1,
            tiled=True,
        ),
    )
    back_in = back_in.reshape(slots, width)[slot]
    back_out = back_out.reshape(slots, width)[slot]
    gate_grad = jnp.sum(out_grad.astype(jnp.float32) * back_out.astype(jnp.float32), axis=1)
    logit_grad = ((gate_grad * gate)[:, None] * (chosen - probs)).astype(jnp.bfloat16)
    columns = logit_grad
    router_part = jnp.dot(
        columns,
        lax.all_gather(router_weight, ("row", "col"), axis=0, tiled=True),
        preferred_element_type=jnp.float32,
    )
    d_tokens = (back_in.astype(jnp.float32) + router_part).astype(jnp.bfloat16)
    columns = logit_grad
    d_router = lax.psum_scatter(
        jnp.dot(columns.T, tokens, preferred_element_type=jnp.float32),
        ("row", "col"),
        scatter_dimension=0,
        tiled=True,
    )
    return (d_tokens, grad_inner[None], grad_outer[None], d_router)


def solution(mesh):
    placed = (
        P(("row", "col"), None),
        P(("row", "col"), None),
        P(("row", "col")),
        P(("row", "col"), None),
        P(("row", "col"), None),
        P(("row", "col"), None, None),
        P(("row", "col"), None, None),
    )
    return jax.shard_map(
        per_device,
        mesh=mesh,
        in_specs=placed,
        out_specs=(
            P(("row", "col"), None),
            P(("row", "col"), None, None),
            P(("row", "col"), None, None),
            P(("row", "col"), None),
        ),
        check_vma=False,
    )
```

profile of v0, /device:TPU:1, one launch (start us, length us, event | category | flops | bytes accessed | tf_op | source)
XLA Modules:
  0.0 370.2 jit_solution(9983804308069617289)
XLA Ops:
  13.1 2.5 scatter_custom_fusion.1
  16.8 5.9 %all-to-all-start.2 = ((bf16[4,32,4,1024]{3,2,1,0:T(4,128)(2,1)}), bf16[4,32,4,1024]{3,2,1,0:T(4,128)(2,1)S(1)}, u32[]{:S(2)}, u32[]{:S(2)}) async-start(bf16[4,32,4,1024]{3,2,1,0:T(4,128)(2,1)} %reshape.59), calls=%async_computation.2 | async-start | bytes 2097152 | tf_op jit(solution)/shard_map/all_to_all | solution.py:69
  22.6 2.4 scatter_custom_fusion
  26.3 10.6 %all-to-all-done.2 = bf16[4,32,4,1024]{3,2,1,0:T(4,128)(2,1)S(1)} async-done(((bf16[4,32,4,1024]{3,2,1,0:T(4,128)(2,1)}), bf16[4,32,4,1024]{3,2,1,0:T(4,128)(2,1)S(1)}, u32[]{:S(2)}, u32[]{:S(2)}) %all-to-all-start.2) | async-done | bytes 1048608 | tf_op jit(solution)/shard_map/all_to_all | solution.py:69
  36.8 3.5 all-to-all-start
  40.4 1.5 copy.35
  41.9 11.7 %all-to-all-done = bf16[4,32,4,1024]{3,2,1,0:T(4,128)(2,1)S(1)} async-done(((bf16[4,32,4,1024]{3,2,1,0:T(4,128)(2,1)}), bf16[4,32,4,1024]{3,2,1,0:T(4,128)(2,1)S(1)}, u32[]{:S(2)}, u32[]{:S(2)}) %all-to-all-start) | async-done | bytes 1048608 | tf_op jit(solution)/shard_map/all_to_all | solution.py:56
  53.6 9.9 %all-to-all-start.3 = ((bf16[4,32,4,1024]{3,2,0,1:T(4,128)(2,1)}), bf16[4,32,4,1024]{3,2,0,1:T(4,128)(2,1)S(1)}, u32[]{:S(2)}, u32[]{:S(2)}) async-start(bf16[4,32,4,1024]{3,2,0,1:T(4,128)(2,1)} %copy.35), calls=%async_computation.3 | async-start | bytes 2097152 | tf_op jit(solution)/shard_map/all_to_all | solution.py:68
  63.5 1.5 copy.33
  65.0 15.4 %all-to-all-done.3 = bf16[4,32,4,1024]{3,2,0,1:T(4,128)(2,1)S(1)} async-done(((bf16[4,32,4,1024]{3,2,0,1:T(4,128)(2,1)}), bf16[4,32,4,1024]{3,2,0,1:T(4,128)(2,1)S(1)}, u32[]{:S(2)}, u32[]{:S(2)}) %all-to-all-start.3) | async-done | bytes 1048608 | tf_op jit(solution)/shard_map/all_to_all | solution.py:68
  80.4 4.0 %all-to-all-start.1 = ((bf16[4,32,4,1024]{3,2,0,1:T(4,128)(2,1)}), bf16[4,32,4,1024]{3,2,0,1:T(4,128)(2,1)S(1)}, u32[]{:S(2)}, u32[]{:S(2)}) async-start(bf16[4,32,4,1024]{3,2,0,1:T(4,128)(2,1)} %copy.33), calls=%async_computation.1 | async-start | bytes 2097152 | tf_op jit(solution)/shard_map/all_to_all | solution.py:55
  85.9 15.4 %all-to-all-done.1 = bf16[4,32,4,1024]{3,2,0,1:T(4,128)(2,1)S(1)} async-done(((bf16[4,32,4,1024]{3,2,0,1:T(4,128)(2,1)}), bf16[4,32,4,1024]{3,2,0,1:T(4,128)(2,1)S(1)}, u32[]{:S(2)}, u32[]{:S(2)}) %all-to-all-start.1) | async-done | bytes 1048608 | tf_op jit(solution)/shard_map/all_to_all | solution.py:55
  102.0 4.9 %fusion.6 = f32[512,2048]{1,0:T(8,128)S(1)} fusion(bf16[512,1024]{1,0:T(8,128)(2,1)S(1)} %reshape.58, bf16[1,1024,2048]{2,1,0:T(8,128)(2,1)} %param.12), kind=kOutput, calls=%fused_computation.10 | convolution fusion | flops 2147483648 | bytes 9437184 | tf_op jit(solution)/shard_map/dot_general | solution.py:17
  106.9 2.0 copy-done.9
  108.9 2.4 fusion.13
  112.5 3.7 all-to-all-start.6
  116.3 6.0 %select_convert_fusion = bf16[512,2048]{1,0:T(8,128)(2,1)S(1)} fusion(f32[512,2048]{1,0:T(8,128)} %copy-done.9, bf16[512,1024]{1,0:T(8,128)(2,1)S(1)} %copy-done.3, bf16[1,2048,1024]{2,1,0:T(8,128)(2,1)} %param.13), kind=kOutput, calls=%fused_computation.15 | convolution fusion | flops 2150629376 | bytes 11534336 | tf_op jit(solution)/shard_map/dot_general | solution.py:22
  122.2 1.3 copy-done.10
  123.6 2.4 fusion.10
  127.2 3.9 %all-to-all-done.6 = bf16[4,32,4,1024]{3,2,1,0:T(4,128)(2,1)S(1)} async-done(((bf16[4,32,4,1024]{3,2,1,0:T(4,128)(2,1)}), bf16[4,32,4,1024]{3,2,1,0:T(4,128)(2,1)S(1)}, u32[]{:S(2)}, u32[]{:S(2)}) %all-to-all-start.6) | async-done | bytes 1048608 | tf_op jit(solution)/shard_map/all_to_all | solution.py:105
  131.1 3.5 all-to-all-start.4
  134.6 1.5 copy.39
  136.2 12.6 %all-to-all-done.4 = bf16[4,32,4,1024]{3,2,1,0:T(4,128)(2,1)S(1)} async-done(((bf16[4,32,4,1024]{3,2,1,0:T(4,128)(2,1)}), bf16[4,32,4,1024]{3,2,1,0:T(4,128)(2,1)S(1)}, u32[]{:S(2)}, u32[]{:S(2)}) %all-to-all-start.4) | async-done | bytes 1048608 | tf_op jit(solution)/shard_map/all_to_all | solution.py:92
  148.8 5.4 %all-to-all-start.7 = ((bf16[4,32,4,1024]{3,2,0,1:T(4,128)(2,1)}), bf16[4,32,4,1024]{3,2,0,1:T(4,128)(2,1)S(1)}, u32[]{:S(2)}, u32[]{:S(2)}) async-start(bf16[4,32,4,1024]{3,2,0,1:T(4,128)(2,1)} %copy.39), calls=%async_computation.7 | async-start | bytes 2097152 | tf_op jit(solution)/shard_map/all_to_all | solution.py:104
  154.3 44.7 %all-gather = bf16[128,1,1024]{2,1,0:T(2,128)(2,1)} all-gather(bf16[1,1,1024]{2,1,0:T(2,128)(2,1)S(1)} %bitcast.47), channel_id=1, replica_groups=mesh['row'=4,'col'=32] {'row','col'}, dimensions={0}, use_global_device_ids=true | all-gather | bytes 264192 | tf_op jit(solution)/shard_map/all_gather | solution.py:125
  199.0 1.5 copy.37
  200.5 4.8 %all-to-all-start.5 = ((bf16[4,32,4,1024]{3,2,0,1:T(4,128)(2,1)}), bf16[4,32,4,1024]{3,2,0,1:T(4,128)(2,1)S(1)}, u32[]{:S(2)}, u32[]{:S(2)}) async-start(bf16[4,32,4,1024]{3,2,0,1:T(4,128)(2,1)} %copy.37), calls=%async_computation.5 | async-start | bytes 2097152 | tf_op jit(solution)/shard_map/all_to_all | solution.py:91
  205.6 6.6 %convert_bitcast_fusion = bf16[1,2048,1024]{2,1,0:T(8,128)(2,1)} fusion(bf16[512,1024]{1,0:T(8,128)(2,1)S(1)} %copy-done.3, f32[512,2048]{1,0:T(8,128)} %copy-done.9), kind=kOutput, calls=%fused_computation.12 | convolution fusion | flops 2151677952 | bytes 9437184 | tf_op jit(solution)/shard_map/dot_general | solution.py:34
  214.4 2.3 fusion.41
  216.7 6.3 %convert_bitcast_fusion.1 = bf16[1,1024,2048]{2,1,0:T(8,128)(2,1)} fusion(bf16[512,1024]{1,0:T(8,128)(2,1)} %copy-done.2, bf16[512,2048]{1,0:T(8,128)(2,1)} %copy-done.10), kind=kOutput, calls=%fused_computation.13 | convolution fusion | flops 2149580800 | bytes 7340032 | tf_op jit(solution)/shard_map/dot_general | solution.py:31
  226.1 135.9 %all-reduce.3.cloned.1.call-done = f32[128,1024]{1,0:T(8,128)} async-done(((f32[128,1024]{1,0:T(8,128)}), f32[128,1024]{1,0:T(8,128)}) %all-reduce.3.cloned.1.call-update) | async-done | bytes 524304
  362.0 1.4 constant_dynamic-slice_fusion
  (55 shorter events, 18.4 us)
Async XLA Ops:
  16.8 20.0 %all-to-all-start.2 = ((bf16[4,32,4,1024]{3,2,1,0:T(4,128)(2,1)}), bf16[4,32,4,1024]{3,2,1,0:T(4,128)(2,1)S(1)}, u32[]{:S(2)}, u32[]{:S(2)}) async-start(bf16[4,32,4,1024]{3,2,1,0:T(4,128)(2,1)} %reshape.59), calls=%async_computation.2 | async-start | bytes 2097152 | tf_op jit(solution)/shard_map/all_to_all | solution.py:69
  36.8 16.8 %all-to-all-start = ((bf16[4,32,4,1024]{3,2,1,0:T(4,128)(2,1)}), bf16[4,32,4,1024]{3,2,1,0:T(4,128)(2,1)S(1)}, u32[]{:S(2)}, u32[]{:S(2)}) async-start(bf16[4,32,4,1024]{3,2,1,0:T(4,128)(2,1)} %reshape.57), calls=%async_computation | async-start | bytes 2097152 | tf_op jit(solution)/shard_map/all_to_all | solution.py:56
  53.6 26.8 %all-to-all-start.3 = ((bf16[4,32,4,1024]{3,2,0,1:T(4,128)(2,1)}), bf16[4,32,4,1024]{3,2,0,1:T(4,128)(2,1)S(1)}, u32[]{:S(2)}, u32[]{:S(2)}) async-start(bf16[4,32,4,1024]{3,2,0,1:T(4,128)(2,1)} %copy.35), calls=%async_computation.3 | async-start | bytes 2097152 | tf_op jit(solution)/shard_map/all_to_all | solution.py:68
  80.4 20.9 %all-to-all-start.1 = ((bf16[4,32,4,1024]{3,2,0,1:T(4,128)(2,1)}), bf16[4,32,4,1024]{3,2,0,1:T(4,128)(2,1)S(1)}, u32[]{:S(2)}, u32[]{:S(2)}) async-start(bf16[4,32,4,1024]{3,2,0,1:T(4,128)(2,1)} %copy.33), calls=%async_computation.1 | async-start | bytes 2097152 | tf_op jit(solution)/shard_map/all_to_all | solution.py:55
  101.9 5.0 %copy-start.2 = (bf16[512,1024]{1,0:T(8,128)(2,1)}, bf16[512,1024]{1,0:T(8,128)(2,1)S(1)}, u32[]{:S(2)}) copy-start(bf16[512,1024]{1,0:T(8,128)(2,1)S(1)} %reshape.58) | copy-start | bytes 3145732
  102.0 7.0 %copy-start.7 = (bf16[1,2048,1024]{2,1,0:T(8,128)(2,1)S(1)}, bf16[1,2048,1024]{2,1,0:T(8,128)(2,1)}, u32[]{:S(2)}) copy-start(bf16[1,2048,1024]{2,1,0:T(8,128)(2,1)} %param.13) | copy-start | bytes 12582916
  106.9 2.0 copy-start.9
  111.3 4.9 %copy-start.3 = (bf16[512,1024]{1,0:T(8,128)(2,1)S(1)}, bf16[512,1024]{1,0:T(8,128)(2,1)}, u32[]{:S(2)}) copy-start(bf16[512,1024]{1,0:T(8,128)(2,1)} %reshape.60) | copy-start | bytes 3145732
  112.5 18.6 %all-to-all-start.6 = ((bf16[4,32,4,1024]{3,2,1,0:T(4,128)(2,1)}), bf16[4,32,4,1024]{3,2,1,0:T(4,128)(2,1)S(1)}, u32[]{:S(2)}, u32[]{:S(2)}) async-start(bf16[4,32,4,1024]{3,2,1,0:T(4,128)(2,1)} %reshape.63), calls=%async_computation.6 | async-start | bytes 2097152 | tf_op jit(solution)/shard_map/all_to_all | solution.py:105
  116.2 7.3 %copy-start.8 = (bf16[1,1024,2048]{2,1,0:T(8,128)(2,1)S(1)}, bf16[1,1024,2048]{2,1,0:T(8,128)(2,1)}, u32[]{:S(2)}) copy-start(bf16[1,1024,2048]{2,1,0:T(8,128)(2,1)} %param.12) | copy-start | bytes 12582916
  122.2 1.3 copy-start.10
  126.0 28.3 %copy-start.6 = (bf16[1,1024]{1,0:T(2,128)(2,1)S(1)}, bf16[1,1024]{1,0:T(2,128)(2,1)}, u32[]{:S(2)}) copy-start(bf16[1,1024]{1,0:T(2,128)(2,1)} %param.11) | copy-start | bytes 6148
  131.1 17.7 %all-to-all-start.4 = ((bf16[4,32,4,1024]{3,2,1,0:T(4,128)(2,1)}), bf16[4,32,4,1024]{3,2,1,0:T(4,128)(2,1)S(1)}, u32[]{:S(2)}, u32[]{:S(2)}) async-start(bf16[4,32,4,1024]{3,2,1,0:T(4,128)(2,1)} %reshape.61), calls=%async_computation.4 | async-start | bytes 2097152 | tf_op jit(solution)/shard_map/all_to_all | solution.py:92
  148.8 51.7 %all-to-all-start.7 = ((bf16[4,32,4,1024]{3,2,0,1:T(4,128)(2,1)}), bf16[4,32,4,1024]{3,2,0,1:T(4,128)(2,1)S(1)}, u32[]{:S(2)}, u32[]{:S(2)}) async-start(bf16[4,32,4,1024]{3,2,0,1:T(4,128)(2,1)} %copy.39), calls=%async_computation.7 | async-start | bytes 2097152 | tf_op jit(solution)/shard_map/all_to_all | solution.py:104
  200.5 22.5 %all-to-all-start.5 = ((bf16[4,32,4,1024]{3,2,0,1:T(4,128)(2,1)}), bf16[4,32,4,1024]{3,2,0,1:T(4,128)(2,1)S(1)}, u32[]{:S(2)}, u32[]{:S(2)}) async-start(bf16[4,32,4,1024]{3,2,0,1:T(4,128)(2,1)} %copy.37), calls=%async_computation.5 | async-start | bytes 2097152 | tf_op jit(solution)/shard_map/all_to_all | solution.py:91
  205.3 156.7 %all-reduce.3.cloned.1.call-start = ((), (), s32[]{:S(2)}) async-start(), calls=%async_computation.8 | async-start | bytes 1048576
  212.6 1.7 copy-start.1
  212.6 1.7 copy-start.5
  212.9 1.2 copy-start
  223.0 1.9 copy-start.4
Sparse Core Ops, SparseCore 0:
  216.8 145.1 all-reduce.2
where the time goes:
time: 371 us; the launch traced here: 370 us
  waiting for transfers between devices  205 us (55%)
  blocking collectives  44.7 us (12%)
  starting transfers between devices  40.9 us (11%)
  matrix products  32 us (9%)
  local copies, waits for them, and re-layouts  24.9 us (7%)
  between operations  14.4 us (4%)
  other arithmetic  7.78 us (2%)
    unnamed x2, waiting for transfers between devices  136 us
    all_gather x1, blocking collectives, per_device(): lax.all_gather(router_weight, ('row', 'col'), axis=0, tiled=True)  44.7 us
    all_to_all x1, waiting for transfers between devices, per_device(): lax.all_to_all(lax.all_to_all(send_rows.reshape(n_row, n_col, capacity, w...  15.4 us
    all_to_all x1, waiting for transfers between devices, per_device(): lax.all_to_all(lax.all_to_all(send_second.reshape(n_row, n_col, capacity,...  15.4 us
    all_to_all x1, waiting for transfers between devices, per_device(): lax.all_to_all(grad_in.reshape(n_row, n_col, capacity, width), 'row', spl...  12.6 us
    all_to_all x1, waiting for transfers between devices, per_device(): lax.all_to_all(send_rows.reshape(n_row, n_col, capacity, width), 'row', s...  11.7 us
    all_to_all x1, waiting for transfers between devices, per_device(): lax.all_to_all(send_second.reshape(n_row, n_col, capacity, width), 'row',...  10.6 us
    all_to_all x1, starting transfers between devices, per_device(): lax.all_to_all(lax.all_to_all(send_second.reshape(n_row, n_col, capacity,...  9.87 us
  transfers between devices with their start and end apart: 9, of which 7 were waited for; matrix products, arithmetic and copies ran while one was open for 11% of the time, Pallas kernels for 0%

commit v1 on v0

v1 whole, which is shorter than its diff:
```python
import jax
import jax.numpy as jnp
from jax import lax
from jax.experimental import pallas as pl
from jax.experimental.pallas import tpu as pltpu
from jax.sharding import PartitionSpec as P

BF16 = jnp.bfloat16
F32 = jnp.float32
AXES = ("row", "col")
CAP = 4
EXTRA = 256
VMEM_LIMIT = 48 * 1024 * 1024


def dot(a, b, ca=1, cb=0):
    return lax.dot_general(a, b, (((ca,), (cb,)), ((), ())), preferred_element_type=F32)


def iota(shape, axis):
    return lax.broadcasted_iota(jnp.int32, shape, axis)


def prep_kernel(ids_ref, logits_ref, tok_ref, og_ref, rw_ref, send_ref, slot_ref, rhs_ref, extra_ref):
    step = pl.program_id(0)
    n_tok, width = tok_ref.shape
    experts = logits_ref.shape[1]
    rows = send_ref.shape[0]

    @pl.when(step == 0)
    def _():
        ids = ids_ref[...]
        onehot_t = jnp.where(iota((experts, n_tok), 0) == ids, 1.0, 0.0).astype(F32)
        upper = jnp.where(iota((n_tok, n_tok), 0) < iota((n_tok, n_tok), 1), 1.0, 0.0)
        earlier = dot(onehot_t.astype(BF16), upper.astype(BF16))
        rank = jnp.sum(earlier * onehot_t, axis=0, keepdims=True)
        slot_ref[...] = ids * (2 * CAP) + rank.astype(jnp.int32)
        onehot = onehot_t.T
        logits = logits_ref[...]
        grown = jnp.exp(logits - jnp.max(logits, axis=1, keepdims=True))
        probs = grown / jnp.sum(grown, axis=1, keepdims=True)
        gate = jnp.sum(probs * onehot, axis=1, keepdims=True)
        rhs_ref[pl.ds(0, n_tok), :] = tok_ref[...]
        rhs_ref[pl.ds(n_tok, n_tok), :] = (gate * og_ref[...].astype(F32)).astype(BF16)
        extra_ref[:, 0:experts] = (onehot - probs).astype(BF16)
        extra_ref[:, experts:] = jnp.zeros((n_tok, EXTRA - experts), BF16)

    slot = slot_ref[...]
    row = iota((rows, n_tok), 0) + step * rows
    first = jnp.where(row == slot, 1.0, 0.0).astype(BF16)
    second = jnp.where(row == slot + CAP, 1.0, 0.0).astype(BF16)
    both = jnp.concatenate([first, second], axis=1)
    send_ref[:, 0:width] = dot(both, rhs_ref[...]).astype(BF16)
    router = rw_ref[...].astype(F32)
    place = iota((2 * CAP, EXTRA), 0)
    pieces = jnp.zeros((2 * CAP, EXTRA), F32)
    for k in range(width // EXTRA):
        piece = jnp.broadcast_to(router[:, k * EXTRA : (k + 1) * EXTRA], (2 * CAP, EXTRA))
        pieces = jnp.where(place == k, piece, pieces)
    side = dot(second, extra_ref[...]).reshape(rows // (2 * CAP), 2 * CAP, EXTRA)
    side = side + pieces[None]
    send_ref[:, width:] = side.reshape(rows, EXTRA).astype(BF16)


def prep(ids, logits, tokens, out_grad, router_weight):
    n_tok, width = tokens.shape
    experts = logits.shape[1]
    rows = experts * 2 * CAP
    steps = 4
    whole = lambda i: (0, 0)
    return pl.pallas_call(
        prep_kernel,
        grid=(steps,),
        out_shape=(
            jax.ShapeDtypeStruct((rows, width + EXTRA), BF16),
            jax.ShapeDtypeStruct((1, n_tok), jnp.int32),
        ),
        in_specs=[
            pl.BlockSpec((1, n_tok), whole),
            pl.BlockSpec((n_tok, experts), whole),
            pl.BlockSpec((n_tok, width), whole),
            pl.BlockSpec((n_tok, width), whole),
            pl.BlockSpec((1, width), whole),
        ],
        out_specs=(
            pl.BlockSpec((rows // steps, width + EXTRA), lambda i: (i, 0)),
            pl.BlockSpec((1, n_tok), whole),
        ),
        scratch_shapes=[
            pltpu.VMEM((2 * n_tok, width), BF16),
            pltpu.VMEM((n_tok, EXTRA), BF16),
        ],
        compiler_params=pltpu.CompilerParams(vmem_limit_bytes=VMEM_LIMIT),
    )(ids, logits, tokens, out_grad, router_weight)


def split_halves(block):
    rows, columns = block.shape
    tiles = block.astype(F32).reshape(rows // 16, 2, 8, columns)
    even, odd = tiles[:, 0], tiles[:, 1]
    low = iota(even.shape, 1) < 4
    first = jnp.where(low, even, pltpu.roll(odd, 4, axis=1))
    second = jnp.where(low, pltpu.roll(even, 4, axis=1), odd)
    return first.reshape(rows // 2, columns).astype(BF16), second.reshape(rows // 2, columns).astype(BF16)


def join_halves(first, second):
    rows, columns = first.shape
    a = first.reshape(rows // 8, 8, columns)
    b = second.reshape(rows // 8, 8, columns)
    low = iota(a.shape, 1) < 4
    even = jnp.where(low, a, pltpu.roll(b, 4, axis=1))
    odd = jnp.where(low, pltpu.roll(a, 4, axis=1), b)
    return jnp.stack([even, odd], axis=1).reshape(2 * rows, columns)


def expert_kernel(
    recv_ref, w_in_ref, w_out_ref, back_ref, routed_ref, scaled_ref, hidden_ref, hgrad_ref,
    gi_ref, c_ref, part_ref,
):
    step = pl.program_id(0)
    last = pl.num_programs(0) - 1
    rows = routed_ref.shape[0]
    width = w_in_ref.shape[0]
    experts = rows // CAP

    @pl.when(step == 0)
    def _():
        for k in range(0, width + EXTRA, 256):
            first, second = split_halves(recv_ref[:, k : k + 256])
            routed_ref[:, k : k + 256] = first
            scaled_ref[:, k : k + 256] = second

    routed = routed_ref[:, 0:width]
    pre = dot(routed, w_in_ref[...])
    back = dot(scaled_ref[:, 0:width], w_out_ref[...], 1, 1)
    active = pre > 0.0
    hidden = jnp.maximum(pre, 0.0)
    hgrad = jnp.where(active, back, 0.0)
    hidden_ref[...] = hidden.astype(BF16)
    hgrad = hgrad.astype(BF16)
    hgrad_ref[...] = hgrad
    c = jnp.sum(hidden * back, axis=1, keepdims=True)
    gi = dot(hgrad, w_in_ref[...], 1, 1)

    @pl.when(step == 0)
    def _():
        gi_ref[...] = gi
        c_ref[...] = c

    @pl.when(step > 0)
    def _():
        gi_ref[...] += gi
        c_ref[...] += c

    @pl.when(step == last)
    def _():
        q = scaled_ref[:, width : width + experts].astype(F32)
        logit_grad = (c_ref[...] * q).astype(BF16)
        pieces = routed_ref[:, width : width + EXTRA]
        for k in range(width // EXTRA):
            pick = jnp.where(iota((experts, rows), 1) == iota((experts, rows), 0) * CAP + k, 1.0, 0.0)
            router = dot(pick.astype(BF16), pieces).astype(BF16)
            gi_ref[:, k * EXTRA : (k + 1) * EXTRA] += dot(logit_grad, router)
        half = width // 2
        for k in range(0, half, 256):
            joined = join_halves(gi_ref[:, k : k + 256], gi_ref[:, half + k : half + k + 256])
            back_ref[:, k : k + 256] = joined.astype(BF16)
        part = dot(logit_grad, routed, 0, 0)
        for k in range(width // 128):
            part_ref[pl.ds(k, experts, stride=8), :] = part[:, k * 128 : (k + 1) * 128]
        back_ref[:, half:] = part_ref[...].astype(BF16)


def expert(recv, w_in, w_out):
    rows2, columns = recv.shape
    rows = rows2 // 2
    width, inner = w_in.shape
    experts = rows // CAP
    block = 512
    whole = lambda i: (0, 0)
    return pl.pallas_call(
        expert_kernel,
        grid=(inner // block,),
        out_shape=(
            jax.ShapeDtypeStruct((rows2, width // 2 + 128), BF16),
            jax.ShapeDtypeStruct((rows, columns), BF16),
            jax.ShapeDtypeStruct((rows, columns), BF16),
            jax.ShapeDtypeStruct((rows, inner), BF16),
            jax.ShapeDtypeStruct((rows, inner), BF16),
        ),
        in_specs=[
            pl.BlockSpec((rows2, columns), whole),
            pl.BlockSpec((width, block), lambda i: (0, i)),
            pl.BlockSpec((block, width), lambda i: (i, 0)),
        ],
        out_specs=(
            pl.BlockSpec((rows2, width // 2 + 128), whole),
            pl.BlockSpec((rows, columns), whole),
            pl.BlockSpec((rows, columns), whole),
            pl.BlockSpec((rows, block), lambda i: (0, i)),
            pl.BlockSpec((rows, block), lambda i: (0, i)),
        ),
        scratch_shapes=[
            pltpu.VMEM((rows, width), F32),
            pltpu.VMEM((rows, 1), F32),
            pltpu.VMEM((experts * 8, 128), F32),
        ],
        compiler_params=pltpu.CompilerParams(vmem_limit_bytes=VMEM_LIMIT),
    )(recv, w_in, w_out)


def weight_kernel(routed_ref, scaled_ref, hidden_ref, hgrad_ref, d_in_ref, d_out_ref):
    width = d_in_ref.shape[0]
    d_in_ref[...] = dot(routed_ref[:, 0:width], hgrad_ref[...], 0, 0).astype(BF16)
    d_out_ref[...] = dot(hidden_ref[...], scaled_ref[:, 0:width], 0, 0).astype(BF16)


def weight_grads(routed, scaled, hidden, hgrad, width):
    rows, inner = hidden.shape
    block = 512
    whole = lambda i: (0, 0)
    flops = 2 * 2 * rows * inner * width
    moved = 2 * (2 * rows * inner + 2 * rows * width + 2 * inner * width)
    return pl.pallas_call(
        weight_kernel,
        grid=(inner // block,),
        out_shape=(
            jax.ShapeDtypeStruct((width, inner), BF16),
            jax.ShapeDtypeStruct((inner, width), BF16),
        ),
        in_specs=[
            pl.BlockSpec(routed.shape, whole),
            pl.BlockSpec(scaled.shape, whole),
            pl.BlockSpec((rows, block), lambda i: (0, i)),
            pl.BlockSpec((rows, block), lambda i: (0, i)),
        ],
        out_specs=(
            pl.BlockSpec((width, block), lambda i: (0, i)),
            pl.BlockSpec((block, width), lambda i: (i, 0)),
        ),
        compiler_params=pltpu.CompilerParams(vmem_limit_bytes=VMEM_LIMIT),
        cost_estimate=pl.CostEstimate(flops=flops, bytes_accessed=moved, transcendentals=0),
    )(routed, scaled, hidden, hgrad)


def post_kernel(recv_ref, slot_ref, d_tok_ref, d_router_ref):
    rows = recv_ref.shape[0]
    n_tok, width = d_tok_ref.shape
    half = width // 2
    row = iota((rows, n_tok), 0)
    slot = slot_ref[...]
    first = jnp.where(row == slot, 1.0, 0.0).astype(BF16)
    second = jnp.where(row == slot + CAP, 1.0, 0.0).astype(BF16)
    d_tok_ref[:, 0:half] = dot(first, recv_ref[:, 0:half], 0, 0).astype(BF16)
    d_tok_ref[:, half:] = dot(second, recv_ref[:, 0:half], 0, 0).astype(BF16)
    parts = recv_ref[:, half:].astype(F32).reshape(rows // 8, 8, 128)
    total = jnp.sum(parts, axis=0)
    for k in range(width // 128):
        d_router_ref[:, k * 128 : (k + 1) * 128] = total[k : k + 1, :]


def post(recv, slot, n_tok, width):
    return pl.pallas_call(
        post_kernel,
        out_shape=(
            jax.ShapeDtypeStruct((n_tok, width), BF16),
            jax.ShapeDtypeStruct((1, width), F32),
        ),
        compiler_params=pltpu.CompilerParams(vmem_limit_bytes=VMEM_LIMIT),
    )(recv, slot)


def exchange(rows, experts):
    count, columns = rows.shape
    cut = rows.reshape(experts, count // experts, columns)
    return lax.all_to_all(cut, AXES, split_axis=0, concat_axis=0, tiled=True).reshape(count, columns)


def per_device(tokens, out_grad, expert_ids, router_logits, router_weight, w_in, w_out):
    experts = router_logits.shape[1]
    n_tok, width = tokens.shape
    send, slot = prep(expert_ids.reshape(1, n_tok), router_logits, tokens, out_grad, router_weight)
    recv = exchange(send, experts)
    ret, routed, scaled, hidden, hgrad = expert(recv, w_in[0], w_out[0])
    got = exchange(ret, experts)
    d_in, d_out = weight_grads(routed, scaled, hidden, hgrad, width)
    d_tokens, d_router = post(got, slot, n_tok, width)
    return (d_tokens, d_in[None], d_out[None], d_router)


def solution(mesh):
    rows = P(AXES, None)
    cube = P(AXES, None, None)
    return jax.shard_map(
        per_device,
        mesh=mesh,
        in_specs=(rows, rows, P(AXES), rows, rows, cube, cube),
        out_specs=(rows, cube, cube, rows),
        check_vma=False,
    )
```

time: 371 us -> 99.4 us (0.27)
  waiting for transfers between devices: 205 us -> 11.8 us
  starting transfers between devices: 40.9 us -> 4.45 us
  matrix products: 32 us -> 0 us
  Pallas kernels: 0 us -> 25.3 us
  local copies, waits for them, and re-layouts: 24.9 us -> 9.08 us
  between operations: 14.4 us -> 0.67 us
  other arithmetic: 7.78 us -> 0 us
    unnamed x2 -> x0, waiting for transfers between devices: 136 us -> none
    all_to_all x8 -> x1, waiting for transfers between devices: 69.6 us -> 11.8 us  [exchange(): lax.all_to_all(cut, AXES, split_axis=0, concat_axis=0, tiled=True)]
    all_to_all x0 -> x1, blocking collectives: none -> 47.5 us  [exchange(): lax.all_to_all(cut, AXES, split_axis=0, concat_axis=0, tiled=True)]
    all_gather x1 -> x0, blocking collectives: 44.7 us -> none  [per_device(): lax.all_gather(router_weight, ('row', 'col'), axis=0, tiled=True)]
    all_to_all x8 -> x1, starting transfers between devices: 40.6 us -> 4.45 us  [exchange(): lax.all_to_all(cut, AXES, split_axis=0, concat_axis=0, tiled=True)]
    dot_general x8 -> x0, matrix products: 32 us -> none  [the longest x1 6.59 us: weight_grads(): jnp.dot(hidden.T, scaled_rows, preferred_element_type=jnp.float32)]
    pallas_call x0 -> x4, Pallas kernels: none -> 25.3 us  [the longest x1 14.1 us: expert(): pl.pallas_call(expert_kernel, grid=(inner // block,), out_shape=(jax.Shap...]
    all_to_all x8 -> x0, local copies, waits for them, and re-layouts: 7.75 us -> none  [the longest x1 1.54 us: per_device(): lax.all_to_all(expert_out.reshape(n_row, n_col, capacity, width), 'row',...]
  transfers between devices with their start and end apart: 9 -> 1, of which waited for: 7 -> 1; matrix products, arithmetic and copies ran while one was open for 11% -> 0% of each run, Pallas kernels for 0% -> 8%
where the time goes in v1:
time: 99.4 us; the launch traced here: 98.8 us
  blocking collectives  47.5 us (48%)
  Pallas kernels  25.3 us (25%)
  waiting for transfers between devices  11.8 us (12%)
  local copies, waits for them, and re-layouts  9.08 us (9%)
  starting transfers between devices  4.45 us (4%)
    all_to_all x1, blocking collectives, exchange(): lax.all_to_all(cut, AXES, split_axis=0, concat_axis=0, tiled=True)  47.5 us
    pallas_call x1, Pallas kernels, expert(): pl.pallas_call(expert_kernel, grid=(inner // block,), out_shape=(jax.Shap...  14.1 us
    all_to_all x1, waiting for transfers between devices, exchange(): lax.all_to_all(cut, AXES, split_axis=0, concat_axis=0, tiled=True)  11.8 us
    unnamed x18, local copies, waits for them, and re-layouts  9.08 us
    pallas_call x1, Pallas kernels, weight_grads(): pl.pallas_call(weight_kernel, grid=(inner // block,), out_shape=(jax.Shap...  7.41 us
    all_to_all x1, starting transfers between devices, exchange(): lax.all_to_all(cut, AXES, split_axis=0, concat_axis=0, tiled=True)  4.45 us
    pallas_call x1, Pallas kernels, prep(): pl.pallas_call(prep_kernel, grid=(steps,), out_shape=(jax.ShapeDtypeStruc...  2.32 us
  transfers between devices with their start and end apart: 1, of which 1 were waited for; matrix products, arithmetic and copies ran while one was open for 0% of the time, Pallas kernels for 8%

profile of v1, /device:TPU:1, one launch (start us, length us, event | category | flops | bytes accessed | tf_op | source)
XLA Modules:
  0.0 98.8 jit_solution(8142880052734853667)
XLA Ops:
  0.6 0.0 copy-start
  0.6 1.0 %copy-done = bf16[256,1024]{1,0:T(8,128)(2,1)S(1)} copy-done((bf16[256,1024]{1,0:T(8,128)(2,1)S(1)}, bf16[256,1024]{1,0:T(8,128)(2,1)}, u32[]{:S(2)}) %copy-start) | copy-done | bytes 524312
  1.7 0.0 copy-start.1
  1.7 1.0 %copy-done.1 = bf16[256,1024]{1,0:T(8,128)(2,1)S(1)} copy-done((bf16[256,1024]{1,0:T(8,128)(2,1)S(1)}, bf16[256,1024]{1,0:T(8,128)(2,1)}, u32[]{:S(2)}) %copy-start.1) | copy-done | bytes 524312
  2.7 0.0 copy-start.2
  2.7 0.9 copy-done.2
  3.6 0.0 copy-start.3
  3.6 0.7 copy-done.3
  4.3 0.0 copy-start.4
  4.3 0.7 copy-done.4
  5.0 2.3 %shard_map.102 = (bf16[1024,1280]{1,0:T(8,128)(2,1)S(1)}, s32[1,256]{1,0:T(1,128)S(1)}) custom-call(s32[1,256]{1,0:T(1,128)S(1)} %bitcast.11, f32[256,128]{1,0:T(8,128)S(1)} %copy-done.2, bf16[256,1024]{1,0:T(8,128)(2,1)S(1)} %copy-done, bf16[256,1024]{1,0:T(8,128)(2,1)S(1)} %copy-done.1, bf16[1,1024]{1,0:T(2,128)(2,1)S(1)} %copy-done.3), custom_call_target="tpu_custom_call" | custom-call | tf_op jit(solution)/shard_map/pallas_call | solution.py:71
  7.3 47.5 %all_to_all.10 = bf16[128,8,1280]{2,1,0:T(8,128)(2,1)} all-to-all(bf16[128,8,1280]{2,1,0:T(8,128)(2,1)S(1)} %bitcast.10), channel_id=1, replica_groups=mesh['row'=4,'col'=32] {'row','col'}, dimensions={0} | all-to-all | bytes 5242880 | tf_op jit(solution)/shard_map/all_to_all | solution.py:277
  54.8 14.1 %shard_map.103 = (bf16[1024,640]{1,0:T(8,128)(2,1)}, bf16[512,1280]{1,0:T(8,128)(2,1)S(1)}, bf16[512,1280]{1,0:T(8,128)(2,1)S(1)}, bf16[512,2048]{1,0:T(8,128)(2,1)S(1)}, bf16[512,2048]{1,0:T(8,128)(2,1)}) custom-call(bf16[1024,1280]{1,0:T(8,128)(2,1)} %bitcast.12, bf16[1024,2048]{1,0:T(8,128)(2,1)} %bitcast.13, bf16[2048,1024]{1,0:T(8,128)(2,1)} %bitcast.14), custom_call_target="tpu_custom_call" | custom-call | tf_op jit(solution)/shard_map/pallas_call | solution.py:182
  68.9 0.0 copy-start.5
  68.9 1.1 %copy-done.5 = bf16[512,1280]{1,0:T(8,128)(2,1)} copy-done((bf16[512,1280]{1,0:T(8,128)(2,1)}, bf16[512,1280]{1,0:T(8,128)(2,1)S(1)}, u32[]{:S(2)}) %copy-start.5) | copy-done | bytes 1310744
  70.0 0.0 copy-start.7
  70.0 1.1 %copy-done.7 = bf16[512,1280]{1,0:T(8,128)(2,1)} copy-done((bf16[512,1280]{1,0:T(8,128)(2,1)}, bf16[512,1280]{1,0:T(8,128)(2,1)S(1)}, u32[]{:S(2)}) %copy-start.7) | copy-done | bytes 1310744
  71.0 4.5 %all-to-all-start.1 = ((bf16[128,8,640]{2,1,0:T(8,128)(2,1)}), bf16[128,8,640]{2,1,0:T(8,128)(2,1)S(1)}, u32[]{:S(2)}, u32[]{:S(2)}) async-start(bf16[128,8,640]{2,1,0:T(8,128)(2,1)} %bitcast.5), calls=%async_computation.1 | async-start | bytes 2621440 | tf_op jit(solution)/shard_map/all_to_all | solution.py:277
  75.5 0.0 copy-start.6
  75.5 1.3 %copy-done.6 = bf16[512,1280]{1,0:T(8,128)(2,1)S(1)} copy-done((bf16[512,1280]{1,0:T(8,128)(2,1)S(1)}, bf16[512,1280]{1,0:T(8,128)(2,1)}, u32[]{:S(2)}) %copy-start.6) | copy-done | bytes 1310744
  76.8 0.0 copy-start.8
  76.8 1.3 %copy-done.8 = bf16[512,1280]{1,0:T(8,128)(2,1)S(1)} copy-done((bf16[512,1280]{1,0:T(8,128)(2,1)S(1)}, bf16[512,1280]{1,0:T(8,128)(2,1)}, u32[]{:S(2)}) %copy-start.8) | copy-done | bytes 1310744
  78.1 7.4 %shard_map.105 = (bf16[1024,2048]{1,0:T(8,128)(2,1)}, bf16[2048,1024]{1,0:T(8,128)(2,1)}) custom-call(bf16[512,1280]{1,0:T(8,128)(2,1)S(1)} %copy-done.6, bf16[512,1280]{1,0:T(8,128)(2,1)S(1)} %copy-done.8, bf16[512,2048]{1,0:T(8,128)(2,1)S(1)} %get-tuple-element.21.hidden_ref, bf16[512,2048]{1,0:T(8,128)(2,1)} %get-tuple-element.22.hgrad_ref), custom_call_target="tpu_custom_call" | custom-call | flops 4294967296 | bytes 14680064 | tf_op jit(solution)/shard_map/pallas_call | solution.py:225
  85.5 11.8 %all-to-all-done.1 = bf16[128,8,640]{2,1,0:T(8,128)(2,1)S(1)} async-done(((bf16[128,8,640]{2,1,0:T(8,128)(2,1)}), bf16[128,8,640]{2,1,0:T(8,128)(2,1)S(1)}, u32[]{:S(2)}, u32[]{:S(2)}) %all-to-all-start.1) | async-done | bytes 1310752 | tf_op jit(solution)/shard_map/all_to_all | solution.py:277
  97.3 1.5 %shard_map.104 = (bf16[256,1024]{1,0:T(8,128)(2,1)}, f32[1,1024]{1,0:T(1,128)}) custom-call(bf16[1024,640]{1,0:T(8,128)(2,1)S(1)} %bitcast.9, s32[1,256]{1,0:T(1,128)S(1)} %get-tuple-element.17.slot_ref), custom_call_target="tpu_custom_call" | custom-call | tf_op jit(solution)/shard_map/pallas_call | solution.py:264
Async XLA Ops:
  0.6 1.0 %copy-start = (bf16[256,1024]{1,0:T(8,128)(2,1)S(1)}, bf16[256,1024]{1,0:T(8,128)(2,1)}, u32[]{:S(2)}) copy-start(bf16[256,1024]{1,0:T(8,128)(2,1)} %tok_ref.1) | copy-start | bytes 1572868
  1.7 1.0 %copy-start.1 = (bf16[256,1024]{1,0:T(8,128)(2,1)S(1)}, bf16[256,1024]{1,0:T(8,128)(2,1)}, u32[]{:S(2)}) copy-start(bf16[256,1024]{1,0:T(8,128)(2,1)} %og_ref.1) | copy-start | bytes 1572868
  2.7 0.9 copy-start.2
  3.6 0.7 copy-start.3
  4.3 0.7 copy-start.4
  68.9 1.1 %copy-start.5 = (bf16[512,1280]{1,0:T(8,128)(2,1)}, bf16[512,1280]{1,0:T(8,128)(2,1)S(1)}, u32[]{:S(2)}) copy-start(bf16[512,1280]{1,0:T(8,128)(2,1)S(1)} %get-tuple-element.19.routed_ref) | copy-start | bytes 3932164
  70.0 1.1 %copy-start.7 = (bf16[512,1280]{1,0:T(8,128)(2,1)}, bf16[512,1280]{1,0:T(8,128)(2,1)S(1)}, u32[]{:S(2)}) copy-start(bf16[512,1280]{1,0:T(8,128)(2,1)S(1)} %get-tuple-element.20.scaled_ref) | copy-start | bytes 3932164
  71.0 26.3 %all-to-all-start.1 = ((bf16[128,8,640]{2,1,0:T(8,128)(2,1)}), bf16[128,8,640]{2,1,0:T(8,128)(2,1)S(1)}, u32[]{:S(2)}, u32[]{:S(2)}) async-start(bf16[128,8,640]{2,1,0:T(8,128)(2,1)} %bitcast.5), calls=%async_computation.1 | async-start | bytes 2621440 | tf_op jit(solution)/shard_map/all_to_all | solution.py:277
  75.5 1.3 %copy-start.6 = (bf16[512,1280]{1,0:T(8,128)(2,1)S(1)}, bf16[512,1280]{1,0:T(8,128)(2,1)}, u32[]{:S(2)}) copy-start(bf16[512,1280]{1,0:T(8,128)(2,1)} %copy-done.5) | copy-start | bytes 3932164
  76.8 1.3 %copy-start.8 = (bf16[512,1280]{1,0:T(8,128)(2,1)S(1)}, bf16[512,1280]{1,0:T(8,128)(2,1)}, u32[]{:S(2)}) copy-start(bf16[512,1280]{1,0:T(8,128)(2,1)} %copy-done.7) | copy-start | bytes 3932164

commit v2 on v1

v2 whole, which is shorter than its diff:
```python
import jax
import jax.numpy as jnp
from jax import lax
from jax.experimental import pallas as pl
from jax.experimental.pallas import tpu as pltpu
from jax.sharding import PartitionSpec as P

BF16 = jnp.bfloat16
F32 = jnp.float32
AXES = ("row", "col")
CAP = 4
EXTRA = 256
MIB = 1024 * 1024
PREP_VMEM = 63 * MIB
EXPERT_VMEM = 56 * MIB
VMEM_LIMIT = 48 * MIB
BLOCKS = 4


def dot(a, b, ca=1, cb=0):
    return lax.dot_general(a, b, (((ca,), (cb,)), ((), ())), preferred_element_type=F32)


def iota(shape, axis):
    return lax.broadcasted_iota(jnp.int32, shape, axis)


def prep_kernel(
    ids_hbm, logits_hbm, tok_hbm, og_hbm, rw_hbm, send_hbm, slot_ref,
    ids_ref, logits_ref, rhs_ref, og_ref, rw_ref, extra_ref, send_ref, sems, out_sems,
):
    n_tok, width = og_ref.shape
    experts = logits_ref.shape[1]
    rows = send_ref.shape[0]
    copies = [
        pltpu.make_async_copy(src, dst, sems.at[i])
        for i, (src, dst) in enumerate(
            [
                (ids_hbm, ids_ref),
                (logits_hbm, logits_ref),
                (og_hbm, og_ref),
                (tok_hbm, rhs_ref.at[pl.ds(0, n_tok), :]),
                (rw_hbm, rw_ref),
            ]
        )
    ]
    for copy in copies:
        copy.start()
    upper = jnp.where(iota((n_tok, n_tok), 0) < iota((n_tok, n_tok), 1), 1.0, 0.0).astype(BF16)
    copies[0].wait()
    ids = ids_ref[...]
    onehot_t = jnp.where(iota((experts, n_tok), 0) == ids, 1.0, 0.0).astype(F32)
    earlier = dot(onehot_t.astype(BF16), upper)
    rank = jnp.sum(earlier * onehot_t, axis=0, keepdims=True)
    slot = ids * (2 * CAP) + rank.astype(jnp.int32)
    slot_ref[...] = slot
    onehot = onehot_t.T
    copies[1].wait()
    logits = logits_ref[...]
    grown = jnp.exp(logits - jnp.max(logits, axis=1, keepdims=True))
    probs = grown / jnp.sum(grown, axis=1, keepdims=True)
    gate = jnp.sum(probs * onehot, axis=1, keepdims=True)
    extra_ref[:, 0:experts] = (onehot - probs).astype(BF16)
    extra_ref[:, experts:] = jnp.zeros((n_tok, EXTRA - experts), BF16)
    copies[2].wait()
    rhs_ref[pl.ds(n_tok, n_tok), :] = (gate * og_ref[...].astype(F32)).astype(BF16)
    copies[3].wait()
    copies[4].wait()
    router = rw_ref[...].astype(F32)
    place = iota((2 * CAP, EXTRA), 0)
    pieces = jnp.zeros((2 * CAP, EXTRA), F32)
    for k in range(width // EXTRA):
        piece = jnp.broadcast_to(router[:, k * EXTRA : (k + 1) * EXTRA], (2 * CAP, EXTRA))
        pieces = jnp.where(place == k, piece, pieces)
    part = rows // 4
    outs = []
    for start in range(0, rows, part):
        row = iota((part, n_tok), 0) + start
        first = jnp.where(row == slot, 1.0, 0.0).astype(BF16)
        second = jnp.where(row == slot + CAP, 1.0, 0.0).astype(BF16)
        both = jnp.concatenate([first, second], axis=1)
        send_ref[start : start + part, 0:width] = dot(both, rhs_ref[...]).astype(BF16)
        side = dot(second, extra_ref[...]).reshape(part // (2 * CAP), 2 * CAP, EXTRA)
        side = side + pieces[None]
        send_ref[start : start + part, width:] = side.reshape(part, EXTRA).astype(BF16)
        out = pltpu.make_async_copy(
            send_ref.at[pl.ds(start, part), :],
            send_hbm.at[pl.ds(start, part), :],
            out_sems.at[start // part],
        )
        out.start()
        outs.append(out)
    for out in outs:
        out.wait()


def prep(ids, logits, tokens, out_grad, router_weight):
    n_tok, width = tokens.shape
    experts = logits.shape[1]
    rows = experts * 2 * CAP
    return pl.pallas_call(
        prep_kernel,
        out_shape=(
            jax.ShapeDtypeStruct((rows, width + EXTRA), BF16),
            jax.ShapeDtypeStruct((1, n_tok), jnp.int32),
        ),
        in_specs=[pl.BlockSpec(memory_space=pltpu.HBM)] * 5,
        out_specs=(
            pl.BlockSpec(memory_space=pltpu.HBM),
            pl.BlockSpec(memory_space=pltpu.VMEM),
        ),
        scratch_shapes=[
            pltpu.VMEM((1, n_tok), jnp.int32),
            pltpu.VMEM((n_tok, experts), F32),
            pltpu.VMEM((2 * n_tok, width), BF16),
            pltpu.VMEM((n_tok, width), BF16),
            pltpu.VMEM((1, width), BF16),
            pltpu.VMEM((n_tok, EXTRA), BF16),
            pltpu.VMEM((rows, width + EXTRA), BF16),
            pltpu.SemaphoreType.DMA((5,)),
            pltpu.SemaphoreType.DMA((4,)),
        ],
        compiler_params=pltpu.CompilerParams(vmem_limit_bytes=PREP_VMEM),
    )(ids, logits, tokens, out_grad, router_weight)


def split_halves(block):
    rows, columns = block.shape
    tiles = block.astype(F32).reshape(rows // 16, 2, 8, columns)
    even, odd = tiles[:, 0], tiles[:, 1]
    low = iota(even.shape, 1) < 4
    first = jnp.where(low, even, pltpu.roll(odd, 4, axis=1))
    second = jnp.where(low, pltpu.roll(even, 4, axis=1), odd)
    return first.reshape(rows // 2, columns).astype(BF16), second.reshape(rows // 2, columns).astype(BF16)


def join_halves(first, second):
    rows, columns = first.shape
    a = first.reshape(rows // 8, 8, columns)
    b = second.reshape(rows // 8, 8, columns)
    low = iota(a.shape, 1) < 4
    even = jnp.where(low, a, pltpu.roll(b, 4, axis=1))
    odd = jnp.where(low, pltpu.roll(a, 4, axis=1), b)
    return jnp.stack([even, odd], axis=1).reshape(2 * rows, columns)


def expert_kernel(
    recv_ref, w_in_hbm, w_out_hbm, back_hbm, routed_hbm, scaled_hbm, hidden_hbm, hgrad_hbm,
    w_in_ref, w_out_ref, back_ref, routed_ref, scaled_ref, hidden_ref, hgrad_ref, part_ref,
    in_sems, out_sems,
):
    rows = routed_ref.shape[0]
    width, inner = w_in_ref.shape
    experts = rows // CAP
    half = width // 2
    block = inner // BLOCKS
    loads = []
    for i in range(BLOCKS):
        cut = pl.ds(i * block, block)
        loads.append(
            (
                pltpu.make_async_copy(w_in_hbm.at[0, :, cut], w_in_ref.at[:, cut], in_sems.at[0, i]),
                pltpu.make_async_copy(w_out_hbm.at[0, cut, :], w_out_ref.at[cut, :], in_sems.at[1, i]),
            )
        )
    for pair in loads:
        for load in pair:
            load.start()
    stores = []

    def store(src, dst):
        copy = pltpu.make_async_copy(src, dst, out_sems.at[len(stores)])
        copy.start()
        stores.append(copy)

    for k in range(0, width + EXTRA, 256):
        first, second = split_halves(recv_ref[:, k : k + 256])
        routed_ref[:, k : k + 256] = first
        scaled_ref[:, k : k + 256] = second
    store(routed_ref.at[:, pl.ds(0, width)], routed_hbm)
    store(scaled_ref.at[:, pl.ds(0, width)], scaled_hbm)
    c = jnp.zeros((rows, 1), F32)
    for i in range(BLOCKS):
        k = i * block
        loads[i][0].wait()
        pre = dot(routed_ref[:, 0:width], w_in_ref[:, k : k + block])
        loads[i][1].wait()
        back = dot(scaled_ref[:, 0:width], w_out_ref[k : k + block, :], 1, 1)
        hidden = jnp.maximum(pre, 0.0)
        hidden_ref[:, k : k + block] = hidden.astype(BF16)
        hgrad_ref[:, k : k + block] = jnp.where(pre > 0.0, back, 0.0).astype(BF16)
        c = c + jnp.sum(hidden * back, axis=1, keepdims=True)
        cut = pl.ds(k, block)
        store(hidden_ref.at[:, cut], hidden_hbm.at[:, cut])
        store(hgrad_ref.at[:, cut], hgrad_hbm.at[:, cut])
    q = scaled_ref[:, width : width + experts].astype(F32)
    logit_grad = (c * q).astype(BF16)
    part = dot(logit_grad, routed_ref[:, 0:width], 0, 0)
    for k in range(width // 128):
        part_ref[pl.ds(k, experts, stride=8), :] = part[:, k * 128 : (k + 1) * 128]
    back_ref[:, half:] = part_ref[...].astype(BF16)
    store(back_ref.at[:, pl.ds(half, 128)], back_hbm.at[:, pl.ds(half, 128)])
    pieces = routed_ref[:, width : width + EXTRA]

    def grad_piece(k):
        pick = jnp.where(iota((experts, rows), 1) == iota((experts, rows), 0) * CAP + k, 1.0, 0.0)
        router = dot(pick.astype(BF16), pieces).astype(BF16)
        grad = dot(hgrad_ref[...], w_in_ref[k * EXTRA : (k + 1) * EXTRA, :], 1, 1)
        return grad + dot(logit_grad, router)

    for k in range(half // EXTRA):
        joined = join_halves(grad_piece(k), grad_piece(half // EXTRA + k))
        back_ref[:, k * EXTRA : (k + 1) * EXTRA] = joined.astype(BF16)
        cut = pl.ds(k * EXTRA, EXTRA)
        store(back_ref.at[:, cut], back_hbm.at[:, cut])
    for copy in stores:
        copy.wait()


def expert(recv, w_in, w_out):
    rows2, columns = recv.shape
    rows = rows2 // 2
    width, inner = w_in.shape[1:]
    experts = rows // CAP
    shapes = [(rows2, width // 2 + 128), (rows, width), (rows, width), (rows, inner), (rows, inner)]
    return pl.pallas_call(
        expert_kernel,
        out_shape=tuple(jax.ShapeDtypeStruct(shape, BF16) for shape in shapes),
        in_specs=[
            pl.BlockSpec(memory_space=pltpu.VMEM),
            pl.BlockSpec(memory_space=pltpu.HBM),
            pl.BlockSpec(memory_space=pltpu.HBM),
        ],
        out_specs=(pl.BlockSpec(memory_space=pltpu.HBM),) * 5,
        scratch_shapes=[
            pltpu.VMEM((width, inner), BF16),
            pltpu.VMEM((inner, width), BF16),
            pltpu.VMEM(shapes[0], BF16),
            pltpu.VMEM((rows, columns), BF16),
            pltpu.VMEM((rows, columns), BF16),
            pltpu.VMEM((rows, inner), BF16),
            pltpu.VMEM((rows, inner), BF16),
            pltpu.VMEM((experts * 8, 128), F32),
            pltpu.SemaphoreType.DMA((2, BLOCKS)),
            pltpu.SemaphoreType.DMA((2 * BLOCKS + 5,)),
        ],
        compiler_params=pltpu.CompilerParams(vmem_limit_bytes=EXPERT_VMEM),
    )(recv, w_in, w_out)


def weight_kernel(routed_ref, scaled_ref, hidden_ref, hgrad_ref, d_in_ref, d_out_ref):
    width = d_in_ref.shape[0]
    d_in_ref[...] = dot(routed_ref[:, 0:width], hgrad_ref[...], 0, 0).astype(BF16)
    d_out_ref[...] = dot(hidden_ref[...], scaled_ref[:, 0:width], 0, 0).astype(BF16)


def weight_grads(routed, scaled, hidden, hgrad, width):
    rows, inner = hidden.shape
    block = 512
    whole = lambda i: (0, 0)
    flops = 2 * 2 * rows * inner * width
    moved = 2 * (2 * rows * inner + 2 * rows * width + 2 * inner * width)
    return pl.pallas_call(
        weight_kernel,
        grid=(inner // block,),
        out_shape=(
            jax.ShapeDtypeStruct((width, inner), BF16),
            jax.ShapeDtypeStruct((inner, width), BF16),
        ),
        in_specs=[
            pl.BlockSpec(routed.shape, whole),
            pl.BlockSpec(scaled.shape, whole),
            pl.BlockSpec((rows, block), lambda i: (0, i)),
            pl.BlockSpec((rows, block), lambda i: (0, i)),
        ],
        out_specs=(
            pl.BlockSpec((width, block), lambda i: (0, i)),
            pl.BlockSpec((block, width), lambda i: (i, 0)),
        ),
        compiler_params=pltpu.CompilerParams(vmem_limit_bytes=VMEM_LIMIT),
        cost_estimate=pl.CostEstimate(flops=flops, bytes_accessed=moved, transcendentals=0),
    )(routed, scaled, hidden, hgrad)


def post_kernel(recv_ref, slot_ref, d_tok_ref, d_router_ref):
    rows = recv_ref.shape[0]
    n_tok, width = d_tok_ref.shape
    half = width // 2
    row = iota((rows, n_tok), 0)
    slot = slot_ref[...]
    first = jnp.where(row == slot, 1.0, 0.0).astype(BF16)
    second = jnp.where(row == slot + CAP, 1.0, 0.0).astype(BF16)
    d_tok_ref[:, 0:half] = dot(first, recv_ref[:, 0:half], 0, 0).astype(BF16)
    d_tok_ref[:, half:] = dot(second, recv_ref[:, 0:half], 0, 0).astype(BF16)
    parts = recv_ref[:, half:].astype(F32).reshape(rows // 8, 8, 128)
    total = jnp.sum(parts, axis=0)
    for k in range(width // 128):
        d_router_ref[:, k * 128 : (k + 1) * 128] = total[k : k + 1, :]


def post(recv, slot, n_tok, width):
    return pl.pallas_call(
        post_kernel,
        out_shape=(
            jax.ShapeDtypeStruct((n_tok, width), BF16),
            jax.ShapeDtypeStruct((1, width), F32),
        ),
        compiler_params=pltpu.CompilerParams(vmem_limit_bytes=VMEM_LIMIT),
    )(recv, slot)


def exchange(rows, experts):
    count, columns = rows.shape
    cut = rows.reshape(experts, count // experts, columns)
    return lax.all_to_all(cut, AXES, split_axis=0, concat_axis=0, tiled=True).reshape(count, columns)


def per_device(tokens, out_grad, expert_ids, router_logits, router_weight, w_in, w_out):
    experts = router_logits.shape[1]
    n_tok, width = tokens.shape
    send, slot = prep(expert_ids.reshape(1, n_tok), router_logits, tokens, out_grad, router_weight)
    recv = exchange(send, experts)
    ret, routed, scaled, hidden, hgrad = expert(recv, w_in, w_out)
    got = exchange(ret, experts)
    d_in, d_out = weight_grads(routed, scaled, hidden, hgrad, width)
    d_tokens, d_router = post(got, slot, n_tok, width)
    return (d_tokens, d_in[None], d_out[None], d_router)


def solution(mesh):
    rows = P(AXES, None)
    cube = P(AXES, None, None)
    return jax.shard_map(
        per_device,
        mesh=mesh,
        in_specs=(rows, rows, P(AXES), rows, rows, cube, cube),
        out_specs=(rows, cube, cube, rows),
        check_vma=False,
    )
```

time: 99.4 us -> 94.7 us (0.953)
  local copies, waits for them, and re-layouts: 9.08 us -> 2.45 us
  Pallas kernels: 25.3 us -> 26.9 us
    unnamed x18 -> x8, local copies, waits for them, and re-layouts: 9.08 us -> 2.45 us
    pallas_call x2, Pallas kernels: 16.4 us -> 17.9 us  [the longest x1 13.7 us: expert(): pl.pallas_call(expert_kernel, out_shape=tuple((jax.ShapeDtypeStruct(shape...]
where the time goes in v2:
time: 94.7 us; the launch traced here: 94.2 us
  blocking collectives  47.7 us (50%)
  Pallas kernels  26.9 us (28%)
  waiting for transfers between devices  11.9 us (13%)
  starting transfers between devices  4.55 us (5%)
  local copies, waits for them, and re-layouts  2.45 us (3%)
    all_to_all x1, blocking collectives, exchange(): lax.all_to_all(cut, AXES, split_axis=0, concat_axis=0, tiled=True)  47.7 us
    pallas_call x1, Pallas kernels, expert(): pl.pallas_call(expert_kernel, out_shape=tuple((jax.ShapeDtypeStruct(shape...  13.7 us
    all_to_all x1, waiting for transfers between devices, exchange(): lax.all_to_all(cut, AXES, split_axis=0, concat_axis=0, tiled=True)  11.9 us
    pallas_call x1, Pallas kernels, weight_grads(): pl.pallas_call(weight_kernel, grid=(inner // block,), out_shape=(jax.Shap...  7.43 us
    all_to_all x1, starting transfers between devices, exchange(): lax.all_to_all(cut, AXES, split_axis=0, concat_axis=0, tiled=True)  4.55 us
    pallas_call x1, Pallas kernels, prep(): pl.pallas_call(prep_kernel, out_shape=(jax.ShapeDtypeStruct((rows, width...  4.18 us
    unnamed x8, local copies, waits for them, and re-layouts  2.45 us
  transfers between devices with their start and end apart: 1, of which 1 were waited for; matrix products, arithmetic and copies ran while one was open for 0% of the time, Pallas kernels for 8%

profile of v2, /device:TPU:1, one launch (start us, length us, event | category | flops | bytes accessed | tf_op | source)
XLA Modules:
  0.0 94.2 jit_solution(13485656354031513926)
XLA Ops:
  0.6 4.2 %shard_map.102 = (bf16[1024,1280]{1,0:T(8,128)(2,1)}, s32[1,256]{1,0:T(1,128)}) custom-call(s32[1,256]{1,0:T(1,128)} %bitcast.11, f32[256,128]{1,0:T(8,128)} %logits_hbm.1, bf16[256,1024]{1,0:T(8,128)(2,1)} %tok_hbm.1, bf16[256,1024]{1,0:T(8,128)(2,1)} %og_hbm.1, bf16[1,1024]{1,0:T(2,128)(2,1)} %rw_hbm.1), custom_call_target="tpu_custom_call" | custom-call | tf_op jit(solution)/shard_map/pallas_call | solution.py:101
  4.8 47.7 %all_to_all.10 = bf16[128,8,1280]{2,1,0:T(8,128)(2,1)} all-to-all(bf16[128,8,1280]{2,1,0:T(8,128)(2,1)} %bitcast.9), channel_id=1, replica_groups=mesh['row'=4,'col'=32] {'row','col'}, dimensions={0} | all-to-all | bytes 5242880 | tf_op jit(solution)/shard_map/all_to_all | solution.py:315
  52.6 13.7 %shard_map.103 = (bf16[1024,640]{1,0:T(8,128)(2,1)}, bf16[512,1024]{1,0:T(8,128)(2,1)}, bf16[512,1024]{1,0:T(8,128)(2,1)}, bf16[512,2048]{1,0:T(8,128)(2,1)}, bf16[512,2048]{1,0:T(8,128)(2,1)}) custom-call(bf16[1024,1280]{1,0:T(8,128)(2,1)} %bitcast.8, bf16[1,1024,2048]{2,1,0:T(8,128)(2,1)} %w_in_hbm.1, bf16[1,2048,1024]{2,1,0:T(8,128)(2,1)} %w_out_hbm.1), custom_call_target="tpu_custom_call" | custom-call | tf_op jit(solution)/shard_map/pallas_call | solution.py:226
  66.3 0.0 copy-start.1
  66.3 4.6 %all-to-all-start.1 = ((bf16[128,8,640]{2,1,0:T(8,128)(2,1)}), bf16[128,8,640]{2,1,0:T(8,128)(2,1)S(1)}, u32[]{:S(2)}, u32[]{:S(2)}) async-start(bf16[128,8,640]{2,1,0:T(8,128)(2,1)} %bitcast.10), calls=%async_computation.1 | async-start | bytes 2621440 | tf_op jit(solution)/shard_map/all_to_all | solution.py:315
  70.9 0.0 copy-done.1
  70.9 0.0 copy-start.2
  70.9 1.2 %copy-done.2 = bf16[512,1024]{1,0:T(8,128)(2,1)S(1)} copy-done((bf16[512,1024]{1,0:T(8,128)(2,1)S(1)}, bf16[512,1024]{1,0:T(8,128)(2,1)}, u32[]{:S(2)}) %copy-start.2) | copy-done | bytes 1048600
  72.1 0.0 copy-start.3
  72.1 1.2 %copy-done.3 = bf16[512,1024]{1,0:T(8,128)(2,1)S(1)} copy-done((bf16[512,1024]{1,0:T(8,128)(2,1)S(1)}, bf16[512,1024]{1,0:T(8,128)(2,1)}, u32[]{:S(2)}) %copy-start.3) | copy-done | bytes 1048600
  73.3 0.0 copy-start
  73.4 7.4 %shard_map.105 = (bf16[1024,2048]{1,0:T(8,128)(2,1)}, bf16[2048,1024]{1,0:T(8,128)(2,1)}) custom-call(bf16[512,1024]{1,0:T(8,128)(2,1)S(1)} %copy-done.2, bf16[512,1024]{1,0:T(8,128)(2,1)S(1)} %copy-done.3, bf16[512,2048]{1,0:T(8,128)(2,1)S(1)} %copy-done.1, bf16[512,2048]{1,0:T(8,128)(2,1)} %get-tuple-element.22.hgrad_ref), custom_call_target="tpu_custom_call" | custom-call | flops 4294967296 | bytes 14680064 | tf_op jit(solution)/shard_map/pallas_call | solution.py:263
  80.8 11.9 %all-to-all-done.1 = bf16[128,8,640]{2,1,0:T(8,128)(2,1)S(1)} async-done(((bf16[128,8,640]{2,1,0:T(8,128)(2,1)}), bf16[128,8,640]{2,1,0:T(8,128)(2,1)S(1)}, u32[]{:S(2)}, u32[]{:S(2)}) %all-to-all-start.1) | async-done | bytes 1310752 | tf_op jit(solution)/shard_map/all_to_all | solution.py:315
  92.7 0.0 copy-done
  92.7 1.5 %shard_map.104 = (bf16[256,1024]{1,0:T(8,128)(2,1)}, f32[1,1024]{1,0:T(1,128)}) custom-call(bf16[1024,640]{1,0:T(8,128)(2,1)S(1)} %bitcast.7, s32[1,256]{1,0:T(1,128)S(1)} %copy-done), custom_call_target="tpu_custom_call" | custom-call | tf_op jit(solution)/shard_map/pallas_call | solution.py:302
Async XLA Ops:
  66.3 4.6 %copy-start.1 = (bf16[512,2048]{1,0:T(8,128)(2,1)S(1)}, bf16[512,2048]{1,0:T(8,128)(2,1)}, u32[]{:S(2)}) copy-start(bf16[512,2048]{1,0:T(8,128)(2,1)} %get-tuple-element.21.hidden_ref) | copy-start | bytes 6291460
  66.3 26.4 %all-to-all-start.1 = ((bf16[128,8,640]{2,1,0:T(8,128)(2,1)}), bf16[128,8,640]{2,1,0:T(8,128)(2,1)S(1)}, u32[]{:S(2)}, u32[]{:S(2)}) async-start(bf16[128,8,640]{2,1,0:T(8,128)(2,1)} %bitcast.10), calls=%async_computation.1 | async-start | bytes 2621440 | tf_op jit(solution)/shard_map/all_to_all | solution.py:315
  70.9 1.2 %copy-start.2 = (bf16[512,1024]{1,0:T(8,128)(2,1)S(1)}, bf16[512,1024]{1,0:T(8,128)(2,1)}, u32[]{:S(2)}) copy-start(bf16[512,1024]{1,0:T(8,128)(2,1)} %get-tuple-element.19.routed_ref) | copy-start | bytes 3145732
  72.1 1.2 %copy-start.3 = (bf16[512,1024]{1,0:T(8,128)(2,1)S(1)}, bf16[512,1024]{1,0:T(8,128)(2,1)}, u32[]{:S(2)}) copy-start(bf16[512,1024]{1,0:T(8,128)(2,1)} %get-tuple-element.20.scaled_ref) | copy-start | bytes 3145732
  73.3 19.4 %copy-start = (s32[1,256]{1,0:T(1,128)S(1)}, s32[1,256]{1,0:T(1,128)}, u32[]{:S(2)}) copy-start(s32[1,256]{1,0:T(1,128)} %get-tuple-element.17.slot_ref) | copy-start | bytes 3076

commit v3 on v2

--- a/solution.py
+++ b/solution.py
@@ -12,8 +12,10 @@
 EXTRA = 256
 MIB = 1024 * 1024
 PREP_VMEM = 63 * MIB
-EXPERT_VMEM = 56 * MIB
-VMEM_LIMIT = 48 * MIB
+EXPERT_VMEM = 46 * MIB
+WEIGHT_VMEM = 50 * MIB
+POST_VMEM = 16 * MIB
+EXPERT_BLOCKS = 1
 BLOCKS = 4
 
 
@@ -145,74 +147,64 @@
 
 
 def expert_kernel(
-    recv_ref, w_in_hbm, w_out_hbm, back_hbm, routed_hbm, scaled_hbm, hidden_hbm, hgrad_hbm,
-    w_in_ref, w_out_ref, back_ref, routed_ref, scaled_ref, hidden_ref, hgrad_ref, part_ref,
-    in_sems, out_sems,
+    recv_ref, w_in_ref, w_out_hbm, back_hbm,
+    w_out_ref, routed_ref, scaled_ref, side_ref, hgrad_ref, back_ref, part_ref, load_sems, sems,
 ):
-    rows = routed_ref.shape[0]
-    width, inner = w_in_ref.shape
+    rows, width = scaled_ref.shape
+    inner = hgrad_ref.shape[1]
     experts = rows // CAP
     half = width // 2
-    block = inner // BLOCKS
+    block = inner // EXPERT_BLOCKS
     loads = []
-    for i in range(BLOCKS):
+    for i in range(EXPERT_BLOCKS):
         cut = pl.ds(i * block, block)
-        loads.append(
-            (
-                pltpu.make_async_copy(w_in_hbm.at[0, :, cut], w_in_ref.at[:, cut], in_sems.at[0, i]),
-                pltpu.make_async_copy(w_out_hbm.at[0, cut, :], w_out_ref.at[cut, :], in_sems.at[1, i]),
-            )
-        )
-    for pair in loads:
-        for load in pair:
-            load.start()
+        load = pltpu.make_async_copy(w_out_hbm.at[0, cut, :], w_out_ref.at[cut, :], load_sems.at[i])
+        load.start()
+        loads.append(load)
     stores = []
 
-    def store(src, dst):
-        copy = pltpu.make_async_copy(src, dst, out_sems.at[len(stores)])
+    def store(start, size):
+        cut = pl.ds(start, size)
+        copy = pltpu.make_async_copy(back_ref.at[:, cut], back_hbm.at[:, cut], sems.at[len(stores)])
         copy.start()
         stores.append(copy)
 
-    for k in range(0, width + EXTRA, 256):
-        first, second = split_halves(recv_ref[:, k : k + 256])
-        routed_ref[:, k : k + 256] = first
-        scaled_ref[:, k : k + 256] = second
-    store(routed_ref.at[:, pl.ds(0, width)], routed_hbm)
-    store(scaled_ref.at[:, pl.ds(0, width)], scaled_hbm)
-    c = jnp.zeros((rows, 1), F32)
-    for i in range(BLOCKS):
+    for k in range(0, width, EXTRA):
+        first, second = split_halves(recv_ref[:, k : k + EXTRA])
+        routed_ref[:, k : k + EXTRA] = first
+        scaled_ref[:, k : k + EXTRA] = second
+    pieces, q = split_halves(recv_ref[:, width:])
+    for i in range(EXTRA // 128):
+        side_ref[i] = pieces[:, i * 128 : (i + 1) * 128].astype(F32)
+    q = q[:, 0:experts].astype(F32)
+    c = jnp.zeros((rows, 128), F32)
+    for i in range(EXPERT_BLOCKS):
         k = i * block
-        loads[i][0].wait()
-        pre = dot(routed_ref[:, 0:width], w_in_ref[:, k : k + block])
-        loads[i][1].wait()
-        back = dot(scaled_ref[:, 0:width], w_out_ref[k : k + block, :], 1, 1)
-        hidden = jnp.maximum(pre, 0.0)
-        hidden_ref[:, k : k + block] = hidden.astype(BF16)
-        hgrad_ref[:, k : k + block] = jnp.where(pre > 0.0, back, 0.0).astype(BF16)
-        c = c + jnp.sum(hidden * back, axis=1, keepdims=True)
-        cut = pl.ds(k, block)
-        store(hidden_ref.at[:, cut], hidden_hbm.at[:, cut])
-        store(hgrad_ref.at[:, cut], hgrad_hbm.at[:, cut])
-    q = scaled_ref[:, width : width + experts].astype(F32)
-    logit_grad = (c * q).astype(BF16)
-    part = dot(logit_grad, routed_ref[:, 0:width], 0, 0)
+        pre = dot(routed_ref[...], w_in_ref[0, :, k : k + block])
+        loads[i].wait()
+        back = dot(scaled_ref[...], w_out_ref[k : k + block, :], 1, 1)
+        hgrad = jnp.where(pre > 0.0, back, 0.0)
+        hgrad_ref[:, k : k + block] = hgrad.astype(BF16)
+        product = pre * hgrad
+        for j in range(0, block, 128):
+            c = c + product[:, j : j + 128]
+    logit_grad = (jnp.sum(c, axis=1, keepdims=True) * q).astype(BF16)
+    part = dot(logit_grad, routed_ref[...], 0, 0)
     for k in range(width // 128):
         part_ref[pl.ds(k, experts, stride=8), :] = part[:, k * 128 : (k + 1) * 128]
     back_ref[:, half:] = part_ref[...].astype(BF16)
-    store(back_ref.at[:, pl.ds(half, 128)], back_hbm.at[:, pl.ds(half, 128)])
-    pieces = routed_ref[:, width : width + EXTRA]
+    store(half, 128)
 
     def grad_piece(k):
-        pick = jnp.where(iota((experts, rows), 1) == iota((experts, rows), 0) * CAP + k, 1.0, 0.0)
-        router = dot(pick.astype(BF16), pieces).astype(BF16)
-        grad = dot(hgrad_ref[...], w_in_ref[k * EXTRA : (k + 1) * EXTRA, :], 1, 1)
+        strips = [side_ref[i, pl.ds(k, experts, stride=CAP), :] for i in range(EXTRA // 128)]
+        router = jnp.concatenate(strips, axis=1).astype(BF16)
+        grad = dot(hgrad_ref[...], w_in_ref[0, k * EXTRA : (k + 1) * EXTRA, :], 1, 1)
         return grad + dot(logit_grad, router)
 
     for k in range(half // EXTRA):
         joined = join_halves(grad_piece(k), grad_piece(half // EXTRA + k))
         back_ref[:, k * EXTRA : (k + 1) * EXTRA] = joined.astype(BF16)
-        cut = pl.ds(k * EXTRA, EXTRA)
-        store(back_ref.at[:, cut], back_hbm.at[:, cut])
+        store(k * EXTRA, EXTRA)
     for copy in stores:
         copy.wait()
 
@@ -222,64 +214,74 @@
     rows = rows2 // 2
     width, inner = w_in.shape[1:]
     experts = rows // CAP
-    shapes = [(rows2, width // 2 + 128), (rows, width), (rows, width), (rows, inner), (rows, inner)]
+    back_shape = (rows2, width // 2 + 128)
     return pl.pallas_call(
         expert_kernel,
-        out_shape=tuple(jax.ShapeDtypeStruct(shape, BF16) for shape in shapes),
+        out_shape=jax.ShapeDtypeStruct(back_shape, BF16),
         in_specs=[
             pl.BlockSpec(memory_space=pltpu.VMEM),
-            pl.BlockSpec(memory_space=pltpu.HBM),
+            pl.BlockSpec(memory_space=pltpu.VMEM),
             pl.BlockSpec(memory_space=pltpu.HBM),
         ],
-        out_specs=(pl.BlockSpec(memory_space=pltpu.HBM),) * 5,
+        out_specs=pl.BlockSpec(memory_space=pltpu.HBM),
         scratch_shapes=[
-            pltpu.VMEM((width, inner), BF16),
             pltpu.VMEM((inner, width), BF16),
-            pltpu.VMEM(shapes[0], BF16),
-            pltpu.VMEM((rows, columns), BF16),
-            pltpu.VMEM((rows, columns), BF16),
+            pltpu.VMEM((rows, width), BF16),
+            pltpu.VMEM((rows, width), BF16),
+            pltpu.VMEM((EXTRA // 128, rows, 128), F32),
             pltpu.VMEM((rows, inner), BF16),
-            pltpu.VMEM((rows, inner), BF16),
+            pltpu.VMEM(back_shape, BF16),
             pltpu.VMEM((experts * 8, 128), F32),
-            pltpu.SemaphoreType.DMA((2, BLOCKS)),
-            pltpu.SemaphoreType.DMA((2 * BLOCKS + 5,)),
+            pltpu.SemaphoreType.DMA((EXPERT_BLOCKS,)),
+            pltpu.SemaphoreType.DMA((width // 2 // EXTRA + 1,)),
         ],
         compiler_params=pltpu.CompilerParams(vmem_limit_bytes=EXPERT_VMEM),
     )(recv, w_in, w_out)
 
 
-def weight_kernel(routed_ref, scaled_ref, hidden_ref, hgrad_ref, d_in_ref, d_out_ref):
-    width = d_in_ref.shape[0]
-    d_in_ref[...] = dot(routed_ref[:, 0:width], hgrad_ref[...], 0, 0).astype(BF16)
-    d_out_ref[...] = dot(hidden_ref[...], scaled_ref[:, 0:width], 0, 0).astype(BF16)
-
-
-def weight_grads(routed, scaled, hidden, hgrad, width):
-    rows, inner = hidden.shape
-    block = 512
-    whole = lambda i: (0, 0)
-    flops = 2 * 2 * rows * inner * width
-    moved = 2 * (2 * rows * inner + 2 * rows * width + 2 * inner * width)
+def weight_kernel(recv_ref, w_in_ref, w_out_ref, d_in_ref, d_out_ref, routed_ref, scaled_ref):
+    width = routed_ref.shape[1]
+
+    @pl.when(pl.program_id(0) == 0)
+    def _():
+        for k in range(0, width, EXTRA):
+            first, second = split_halves(recv_ref[:, k : k + EXTRA])
+            routed_ref[:, k : k + EXTRA] = first
+            scaled_ref[:, k : k + EXTRA] = second
+
+    pre = dot(routed_ref[...], w_in_ref[0])
+    back = dot(scaled_ref[...], w_out_ref[0], 1, 1)
+    hidden = jnp.maximum(pre, 0.0).astype(BF16)
+    hgrad = jnp.where(pre > 0.0, back, 0.0).astype(BF16)
+    d_in_ref[0] = dot(routed_ref[...], hgrad, 0, 0).astype(BF16)
+    d_out_ref[0] = dot(hidden, scaled_ref[...], 0, 0).astype(BF16)
+
+
+def weight_grads(recv, w_in, w_out):
+    rows2, columns = recv.shape
+    rows = rows2 // 2
+    width, inner = w_in.shape[1:]
+    block = inner // BLOCKS
+    flops = 4 * 2 * rows * inner * width
+    moved = 2 * (rows2 * columns + 4 * inner * width)
+    in_block = pl.BlockSpec((1, width, block), lambda i: (0, 0, i))
+    out_block = pl.BlockSpec((1, block, width), lambda i: (0, i, 0))
     return pl.pallas_call(
         weight_kernel,
-        grid=(inner // block,),
+        grid=(BLOCKS,),
         out_shape=(
-            jax.ShapeDtypeStruct((width, inner), BF16),
-            jax.ShapeDtypeStruct((inner, width), BF16),
+            jax.ShapeDtypeStruct(w_in.shape, BF16),
+            jax.ShapeDtypeStruct(w_out.shape, BF16),
         ),
-        in_specs=[
-            pl.BlockSpec(routed.shape, whole),
-            pl.BlockSpec(scaled.shape, whole),
-            pl.BlockSpec((rows, block), lambda i: (0, i)),
-            pl.BlockSpec((rows, block), lambda i: (0, i)),
+        in_specs=[pl.BlockSpec((rows2, columns), lambda i: (0, 0)), in_block, out_block],
+        out_specs=(in_block, out_block),
+        scratch_shapes=[
+            pltpu.VMEM((rows, width), BF16),
+            pltpu.VMEM((rows, width), BF16),
         ],
-        out_specs=(
-            pl.BlockSpec((width, block), lambda i: (0, i)),
-            pl.BlockSpec((block, width), lambda i: (i, 0)),
-        ),
-        compiler_params=pltpu.CompilerParams(vmem_limit_bytes=VMEM_LIMIT),
+        compiler_params=pltpu.CompilerParams(vmem_limit_bytes=WEIGHT_VMEM),
         cost_estimate=pl.CostEstimate(flops=flops, bytes_accessed=moved, transcendentals=0),
-    )(routed, scaled, hidden, hgrad)
+    )(recv, w_in, w_out)
 
 
 def post_kernel(recv_ref, slot_ref, d_tok_ref, d_router_ref):
@@ -305,7 +307,7 @@
             jax.ShapeDtypeStruct((n_tok, width), BF16),
             jax.ShapeDtypeStruct((1, width), F32),
         ),
-        compiler_params=pltpu.CompilerParams(vmem_limit_bytes=VMEM_LIMIT),
+        compiler_params=pltpu.CompilerParams(vmem_limit_bytes=POST_VMEM),
     )(recv, slot)
 
 
@@ -320,11 +322,10 @@
     n_tok, width = tokens.shape
     send, slot = prep(expert_ids.reshape(1, n_tok), router_logits, tokens, out_grad, router_weight)
     recv = exchange(send, experts)
-    ret, routed, scaled, hidden, hgrad = expert(recv, w_in, w_out)
-    got = exchange(ret, experts)
-    d_in, d_out = weight_grads(routed, scaled, hidden, hgrad, width)
+    got = exchange(expert(recv, w_in, w_out), experts)
+    d_in, d_out = weight_grads(recv, w_in, w_out)
     d_tokens, d_router = post(got, slot, n_tok, width)
-    return (d_tokens, d_in[None], d_out[None], d_router)
+    return (d_tokens, d_in, d_out, d_router)
 
 
 def solution(mesh):

time: 94.7 us -> 92 us (0.971)
  waiting for transfers between devices: 11.9 us -> 8.57 us
  Pallas kernels: 26.9 us -> 28.4 us
  local copies, waits for them, and re-layouts: 2.45 us -> 1.08 us
    all_to_all x1, waiting for transfers between devices: 11.9 us -> 8.57 us  [exchange(): lax.all_to_all(cut, AXES, split_axis=0, concat_axis=0, tiled=True)]
    unnamed x8 -> x6, local copies, waits for them, and re-layouts: 2.45 us -> 1.08 us
    pallas_call x1, Pallas kernels: 1.54 us -> 2.86 us  [post(): pl.pallas_call(post_kernel, out_shape=(jax.ShapeDtypeStruct((n_tok, width...]
  transfers between devices with their start and end apart: 1 -> 1, of which waited for: 1 -> 1; matrix products, arithmetic and copies ran while one was open for 0% -> 0% of each run, Pallas kernels for 8% -> 14%
where the time goes in v3:
time: 92 us; the launch traced here: 91.8 us
  blocking collectives  47.6 us (52%)
  Pallas kernels  28.4 us (31%)
  waiting for transfers between devices  8.57 us (9%)
  starting transfers between devices  5.42 us (6%)
  local copies, waits for them, and re-layouts  1.08 us (1%)
    all_to_all x1, blocking collectives, exchange(): lax.all_to_all(cut, AXES, split_axis=0, concat_axis=0, tiled=True)  47.6 us
    pallas_call x1, Pallas kernels, weight_grads(): pl.pallas_call(weight_kernel, grid=(BLOCKS,), out_shape=(jax.ShapeDtypeSt...  12.9 us
    all_to_all x1, waiting for transfers between devices, exchange(): lax.all_to_all(cut, AXES, split_axis=0, concat_axis=0, tiled=True)  8.57 us
    pallas_call x1, Pallas kernels, expert(): pl.pallas_call(expert_kernel, out_shape=jax.ShapeDtypeStruct(back_shape,...  8.44 us
    all_to_all x1, starting transfers between devices, exchange(): lax.all_to_all(cut, AXES, split_axis=0, concat_axis=0, tiled=True)  5.42 us
    pallas_call x1, Pallas kernels, prep(): pl.pallas_call(prep_kernel, out_shape=(jax.ShapeDtypeStruct((rows, width...  4.18 us
    pallas_call x1, Pallas kernels, post(): pl.pallas_call(post_kernel, out_shape=(jax.ShapeDtypeStruct((n_tok, width...  2.86 us
  transfers between devices with their start and end apart: 1, of which 1 were waited for; matrix products, arithmetic and copies ran while one was open for 0% of the time, Pallas kernels for 14%

profile of v3, /device:TPU:1, one launch (start us, length us, event | category | flops | bytes accessed | tf_op | source)
XLA Modules:
  0.0 91.8 jit_solution(3436771286152542373)
XLA Ops:
  0.6 4.2 %shard_map.102 = (bf16[1024,1280]{1,0:T(8,128)(2,1)}, s32[1,256]{1,0:T(1,128)}) custom-call(s32[1,256]{1,0:T(1,128)} %bitcast.9, f32[256,128]{1,0:T(8,128)} %logits_hbm.1, bf16[256,1024]{1,0:T(8,128)(2,1)} %tok_hbm.1, bf16[256,1024]{1,0:T(8,128)(2,1)} %og_hbm.1, bf16[1,1024]{1,0:T(2,128)(2,1)} %rw_hbm.1), custom_call_target="tpu_custom_call" | custom-call | tf_op jit(solution)/shard_map/pallas_call | solution.py:103
  4.8 0.0 copy-start.1
  4.8 47.6 %all_to_all.10 = bf16[128,8,1280]{2,1,0:T(8,128)(2,1)S(1)} all-to-all(bf16[128,8,1280]{2,1,0:T(8,128)(2,1)} %bitcast.8), channel_id=1, replica_groups=mesh['row'=4,'col'=32] {'row','col'}, dimensions={0} | all-to-all | bytes 5242880 | tf_op jit(solution)/shard_map/all_to_all | solution.py:317
  52.5 0.0 copy-done.1
  52.5 8.4 %shard_map.103 = bf16[1024,640]{1,0:T(8,128)(2,1)S(1)} custom-call(bf16[1024,1280]{1,0:T(8,128)(2,1)S(1)} %bitcast.5, bf16[1,1024,2048]{2,1,0:T(8,128)(2,1)S(1)} %copy-done.1, bf16[1,2048,1024]{2,1,0:T(8,128)(2,1)} %w_out_ref.1), custom_call_target="tpu_custom_call" | custom-call | tf_op jit(solution)/shard_map/pallas_call | solution.py:218
  60.9 0.0 copy-start
  60.9 1.1 %copy-done = bf16[1024,640]{1,0:T(8,128)(2,1)} copy-done((bf16[1024,640]{1,0:T(8,128)(2,1)}, bf16[1024,640]{1,0:T(8,128)(2,1)S(1)}, u32[]{:S(2)}) %copy-start) | copy-done | bytes 1310744
  62.0 5.4 %all-to-all-start.1 = ((bf16[128,8,640]{2,1,0:T(8,128)(2,1)}), bf16[128,8,640]{2,1,0:T(8,128)(2,1)}, u32[]{:S(2)}, u32[]{:S(2)}) async-start(bf16[128,8,640]{2,1,0:T(8,128)(2,1)} %bitcast.7), calls=%async_computation.1 | async-start | bytes 2621440 | tf_op jit(solution)/shard_map/all_to_all | solution.py:317
  67.4 0.0 copy-start.2
  67.4 12.9 %shard_map.105 = (bf16[1,1024,2048]{2,1,0:T(8,128)(2,1)}, bf16[1,2048,1024]{2,1,0:T(8,128)(2,1)}) custom-call(bf16[1024,1280]{1,0:T(8,128)(2,1)S(1)} %bitcast.6, bf16[1,1024,2048]{2,1,0:T(8,128)(2,1)} %w_in_ref.3, bf16[1,2048,1024]{2,1,0:T(8,128)(2,1)} %w_out_ref.1), custom_call_target="tpu_custom_call" | custom-call | flops 8589934592 | bytes 19398656 | tf_op jit(solution)/shard_map/pallas_call | solution.py:269
  80.4 8.6 %all-to-all-done.1 = bf16[128,8,640]{2,1,0:T(8,128)(2,1)} async-done(((bf16[128,8,640]{2,1,0:T(8,128)(2,1)}), bf16[128,8,640]{2,1,0:T(8,128)(2,1)}, u32[]{:S(2)}, u32[]{:S(2)}) %all-to-all-start.1) | async-done | bytes 1310752 | tf_op jit(solution)/shard_map/all_to_all | solution.py:317
  88.9 0.0 copy-done.2
  88.9 2.9 %shard_map.104 = (bf16[256,1024]{1,0:T(8,128)(2,1)}, f32[1,1024]{1,0:T(1,128)}) custom-call(bf16[1024,640]{1,0:T(8,128)(2,1)} %bitcast.4.recv_ref, s32[1,256]{1,0:T(1,128)S(1)} %copy-done.2), custom_call_target="tpu_custom_call" | custom-call | tf_op jit(solution)/shard_map/pallas_call | solution.py:304
Async XLA Ops:
  4.8 47.6 %copy-start.1 = (bf16[1,1024,2048]{2,1,0:T(8,128)(2,1)S(1)}, bf16[1,1024,2048]{2,1,0:T(8,128)(2,1)}, u32[]{:S(2)}) copy-start(bf16[1,1024,2048]{2,1,0:T(8,128)(2,1)} %w_in_ref.3) | copy-start | bytes 12582916
  60.9 1.1 %copy-start = (bf16[1024,640]{1,0:T(8,128)(2,1)}, bf16[1024,640]{1,0:T(8,128)(2,1)S(1)}, u32[]{:S(2)}) copy-start(bf16[1024,640]{1,0:T(8,128)(2,1)S(1)} %shard_map.103) | copy-start | bytes 3932164
  62.0 26.9 %all-to-all-start.1 = ((bf16[128,8,640]{2,1,0:T(8,128)(2,1)}), bf16[128,8,640]{2,1,0:T(8,128)(2,1)}, u32[]{:S(2)}, u32[]{:S(2)}) async-start(bf16[128,8,640]{2,1,0:T(8,128)(2,1)} %bitcast.7), calls=%async_computation.1 | async-start | bytes 2621440 | tf_op jit(solution)/shard_map/all_to_all | solution.py:317
  67.4 21.5 %copy-start.2 = (s32[1,256]{1,0:T(1,128)S(1)}, s32[1,256]{1,0:T(1,128)}, u32[]{:S(2)}) copy-start(s32[1,256]{1,0:T(1,128)} %get-tuple-element.11.slot_ref) | copy-start | bytes 3076

commit v4 on v3

--- a/solution.py
+++ b/solution.py
@@ -13,10 +13,11 @@
 MIB = 1024 * 1024
 PREP_VMEM = 63 * MIB
 EXPERT_VMEM = 46 * MIB
-WEIGHT_VMEM = 50 * MIB
+WEIGHT_VMEM = 55 * MIB
 POST_VMEM = 16 * MIB
-EXPERT_BLOCKS = 1
+EXPERT_BLOCKS = 2
 BLOCKS = 4
+PREP_PARTS = 8
 
 
 def dot(a, b, ca=1, cb=0):
@@ -74,7 +75,7 @@
     for k in range(width // EXTRA):
         piece = jnp.broadcast_to(router[:, k * EXTRA : (k + 1) * EXTRA], (2 * CAP, EXTRA))
         pieces = jnp.where(place == k, piece, pieces)
-    part = rows // 4
+    part = rows // PREP_PARTS
     outs = []
     for start in range(0, rows, part):
         row = iota((part, n_tok), 0) + start
@@ -120,7 +121,7 @@
             pltpu.VMEM((n_tok, EXTRA), BF16),
             pltpu.VMEM((rows, width + EXTRA), BF16),
             pltpu.SemaphoreType.DMA((5,)),
-            pltpu.SemaphoreType.DMA((4,)),
+            pltpu.SemaphoreType.DMA((PREP_PARTS,)),
         ],
         compiler_params=pltpu.CompilerParams(vmem_limit_bytes=PREP_VMEM),
     )(ids, logits, tokens, out_grad, router_weight)
@@ -178,9 +179,10 @@
         side_ref[i] = pieces[:, i * 128 : (i + 1) * 128].astype(F32)
     q = q[:, 0:experts].astype(F32)
     c = jnp.zeros((rows, 128), F32)
+    pre_all = dot(routed_ref[...], w_in_ref[0])
     for i in range(EXPERT_BLOCKS):
         k = i * block
-        pre = dot(routed_ref[...], w_in_ref[0, :, k : k + block])
+        pre = pre_all[:, k : k + block]
         loads[i].wait()
         back = dot(scaled_ref[...], w_out_ref[k : k + block, :], 1, 1)
         hgrad = jnp.where(pre > 0.0, back, 0.0)

time: 92 us -> 89.4 us (0.972)
  local copies, waits for them, and re-layouts: 1.08 us -> 0.02 us
  starting transfers between devices: 5.42 us -> 4.42 us
    pallas_call x1, Pallas kernels: 2.86 us -> 1.54 us  [post(): pl.pallas_call(post_kernel, out_shape=(jax.ShapeDtypeStruct((n_tok, width...]
    unnamed x6, local copies, waits for them, and re-layouts: 1.08 us -> 0.02 us
    all_to_all x1, starting transfers between devices: 5.42 us -> 4.42 us  [exchange(): lax.all_to_all(cut, AXES, split_axis=0, concat_axis=0, tiled=True)]
  transfers between devices with their start and end apart: 1 -> 1, of which waited for: 1 -> 1; matrix products, arithmetic and copies ran while one was open for 0% -> 0% of each run, Pallas kernels for 14% -> 15%
where the time goes in v4:
time: 89.4 us; the launch traced here: 89.2 us
  blocking collectives  47.6 us (53%)
  Pallas kernels  28.4 us (32%)
  waiting for transfers between devices  8.04 us (9%)
  starting transfers between devices  4.42 us (5%)
    all_to_all x1, blocking collectives, exchange(): lax.all_to_all(cut, AXES, split_axis=0, concat_axis=0, tiled=True)  47.6 us
    pallas_call x1, Pallas kernels, weight_grads(): pl.pallas_call(weight_kernel, grid=(BLOCKS,), out_shape=(jax.ShapeDtypeSt...  13.8 us
    pallas_call x1, Pallas kernels, expert(): pl.pallas_call(expert_kernel, out_shape=jax.ShapeDtypeStruct(back_shape,...  9.02 us
    all_to_all x1, waiting for transfers between devices, exchange(): lax.all_to_all(cut, AXES, split_axis=0, concat_axis=0, tiled=True)  8.04 us
    all_to_all x1, starting transfers between devices, exchange(): lax.all_to_all(cut, AXES, split_axis=0, concat_axis=0, tiled=True)  4.42 us
    pallas_call x1, Pallas kernels, prep(): pl.pallas_call(prep_kernel, out_shape=(jax.ShapeDtypeStruct((rows, width...  4.11 us
  transfers between devices with their start and end apart: 1, of which 1 were waited for; matrix products, arithmetic and copies ran while one was open for 0% of the time, Pallas kernels for 15%

profile of v4, /device:TPU:1, one launch (start us, length us, event | category | flops | bytes accessed | tf_op | source)
XLA Modules:
  0.0 89.2 jit_solution(3435624600069805206)
XLA Ops:
  0.6 4.1 %shard_map.102 = (bf16[1024,1280]{1,0:T(8,128)(2,1)}, s32[1,256]{1,0:T(1,128)}) custom-call(s32[1,256]{1,0:T(1,128)} %bitcast.9, f32[256,128]{1,0:T(8,128)} %logits_hbm.1, bf16[256,1024]{1,0:T(8,128)(2,1)} %tok_hbm.1, bf16[256,1024]{1,0:T(8,128)(2,1)} %og_hbm.1, bf16[1,1024]{1,0:T(2,128)(2,1)} %rw_hbm.1), custom_call_target="tpu_custom_call" | custom-call | tf_op jit(solution)/shard_map/pallas_call | solution.py:104
  4.8 0.0 copy-start.1
  4.8 47.6 %all_to_all.10 = bf16[128,8,1280]{2,1,0:T(8,128)(2,1)S(1)} all-to-all(bf16[128,8,1280]{2,1,0:T(8,128)(2,1)} %bitcast.8), channel_id=1, replica_groups=mesh['row'=4,'col'=32] {'row','col'}, dimensions={0} | all-to-all | bytes 5242880 | tf_op jit(solution)/shard_map/all_to_all | solution.py:319
  52.4 0.0 copy-start
  52.4 0.0 copy-done.1
  52.4 9.0 %shard_map.103 = bf16[1024,640]{1,0:T(8,128)(2,1)} custom-call(bf16[1024,1280]{1,0:T(8,128)(2,1)S(1)} %bitcast.5, bf16[1,1024,2048]{2,1,0:T(8,128)(2,1)S(1)} %copy-done.1, bf16[1,2048,1024]{2,1,0:T(8,128)(2,1)} %w_out_ref.1), custom_call_target="tpu_custom_call" | custom-call | tf_op jit(solution)/shard_map/pallas_call | solution.py:220
  61.4 0.0 copy-done
  61.4 4.4 %all-to-all-start.1 = ((bf16[128,8,640]{2,1,0:T(8,128)(2,1)}), bf16[128,8,640]{2,1,0:T(8,128)(2,1)S(1)}, u32[]{:S(2)}, u32[]{:S(2)}) async-start(bf16[128,8,640]{2,1,0:T(8,128)(2,1)} %bitcast.3), calls=%async_computation.1 | async-start | bytes 2621440 | tf_op jit(solution)/shard_map/all_to_all | solution.py:319
  65.9 0.0 copy-start.2
  65.9 13.8 %shard_map.105 = (bf16[1,1024,2048]{2,1,0:T(8,128)(2,1)}, bf16[1,2048,1024]{2,1,0:T(8,128)(2,1)}) custom-call(bf16[1024,1280]{1,0:T(8,128)(2,1)} %bitcast.6, bf16[1,1024,2048]{2,1,0:T(8,128)(2,1)} %w_in_ref.3, bf16[1,2048,1024]{2,1,0:T(8,128)(2,1)} %w_out_ref.1), custom_call_target="tpu_custom_call" | custom-call | flops 8589934592 | bytes 19398656 | tf_op jit(solution)/shard_map/pallas_call | solution.py:271
  79.6 8.0 %all-to-all-done.1 = bf16[128,8,640]{2,1,0:T(8,128)(2,1)S(1)} async-done(((bf16[128,8,640]{2,1,0:T(8,128)(2,1)}), bf16[128,8,640]{2,1,0:T(8,128)(2,1)S(1)}, u32[]{:S(2)}, u32[]{:S(2)}) %all-to-all-start.1) | async-done | bytes 1310752 | tf_op jit(solution)/shard_map/all_to_all | solution.py:319
  87.7 0.0 copy-done.2
  87.7 1.5 %shard_map.104 = (bf16[256,1024]{1,0:T(8,128)(2,1)}, f32[1,1024]{1,0:T(1,128)}) custom-call(bf16[1024,640]{1,0:T(8,128)(2,1)S(1)} %bitcast.7, s32[1,256]{1,0:T(1,128)S(1)} %copy-done.2), custom_call_target="tpu_custom_call" | custom-call | tf_op jit(solution)/shard_map/pallas_call | solution.py:306
Async XLA Ops:
  4.8 47.7 %copy-start.1 = (bf16[1,1024,2048]{2,1,0:T(8,128)(2,1)S(1)}, bf16[1,1024,2048]{2,1,0:T(8,128)(2,1)}, u32[]{:S(2)}) copy-start(bf16[1,1024,2048]{2,1,0:T(8,128)(2,1)} %w_in_ref.3) | copy-start | bytes 12582916
  52.4 9.0 %copy-start = (bf16[128,8,1280]{2,1,0:T(8,128)(2,1)}, bf16[128,8,1280]{2,1,0:T(8,128)(2,1)S(1)}, u32[]{:S(2)}) copy-start(bf16[128,8,1280]{2,1,0:T(8,128)(2,1)S(1)} %all_to_all.10) | copy-start | bytes 7864324
  61.4 26.2 %all-to-all-start.1 = ((bf16[128,8,640]{2,1,0:T(8,128)(2,1)}), bf16[128,8,640]{2,1,0:T(8,128)(2,1)S(1)}, u32[]{:S(2)}, u32[]{:S(2)}) async-start(bf16[128,8,640]{2,1,0:T(8,128)(2,1)} %bitcast.3), calls=%async_computation.1 | async-start | bytes 2621440 | tf_op jit(solution)/shard_map/all_to_all | solution.py:319
  65.9 21.8 %copy-start.2 = (s32[1,256]{1,0:T(1,128)S(1)}, s32[1,256]{1,0:T(1,128)}, u32[]{:S(2)}) copy-start(s32[1,256]{1,0:T(1,128)} %get-tuple-element.11.slot_ref) | copy-start | bytes 3076

commit v5 on v4

--- a/solution.py
+++ b/solution.py
@@ -9,7 +9,8 @@
 F32 = jnp.float32
 AXES = ("row", "col")
 CAP = 4
-EXTRA = 256
+EXTRA = 128
+PIECE = 256
 MIB = 1024 * 1024
 PREP_VMEM = 63 * MIB
 EXPERT_VMEM = 46 * MIB
@@ -29,8 +30,8 @@
 
 
 def prep_kernel(
-    ids_hbm, logits_hbm, tok_hbm, og_hbm, rw_hbm, send_hbm, slot_ref,
-    ids_ref, logits_ref, rhs_ref, og_ref, rw_ref, extra_ref, send_ref, sems, out_sems,
+    ids_hbm, logits_hbm, tok_hbm, og_hbm, rw_hbm, send_hbm, slot_ref, q_ref,
+    ids_ref, logits_ref, rhs_ref, og_ref, rw_ref, send_ref, sems, out_sems,
 ):
     n_tok, width = og_ref.shape
     experts = logits_ref.shape[1]
@@ -63,18 +64,19 @@
     grown = jnp.exp(logits - jnp.max(logits, axis=1, keepdims=True))
     probs = grown / jnp.sum(grown, axis=1, keepdims=True)
     gate = jnp.sum(probs * onehot, axis=1, keepdims=True)
-    extra_ref[:, 0:experts] = (onehot - probs).astype(BF16)
-    extra_ref[:, experts:] = jnp.zeros((n_tok, EXTRA - experts), BF16)
+    q = (onehot - probs).astype(BF16)
+    q_ref[...] = q
     copies[2].wait()
     rhs_ref[pl.ds(n_tok, n_tok), :] = (gate * og_ref[...].astype(F32)).astype(BF16)
     copies[3].wait()
     copies[4].wait()
     router = rw_ref[...].astype(F32)
-    place = iota((2 * CAP, EXTRA), 0)
-    pieces = jnp.zeros((2 * CAP, EXTRA), F32)
-    for k in range(width // EXTRA):
-        piece = jnp.broadcast_to(router[:, k * EXTRA : (k + 1) * EXTRA], (2 * CAP, EXTRA))
-        pieces = jnp.where(place == k, piece, pieces)
+    group = 4 * CAP
+    place = iota((group, EXTRA), 0)
+    pieces = jnp.zeros((group, EXTRA), F32)
+    for k in range(2 * CAP):
+        piece = jnp.broadcast_to(router[:, k * EXTRA : (k + 1) * EXTRA], (group, EXTRA))
+        pieces = jnp.where(place == k + k // CAP * CAP, piece, pieces)
     part = rows // PREP_PARTS
     outs = []
     for start in range(0, rows, part):
@@ -83,7 +85,7 @@
         second = jnp.where(row == slot + CAP, 1.0, 0.0).astype(BF16)
         both = jnp.concatenate([first, second], axis=1)
         send_ref[start : start + part, 0:width] = dot(both, rhs_ref[...]).astype(BF16)
-        side = dot(second, extra_ref[...]).reshape(part // (2 * CAP), 2 * CAP, EXTRA)
+        side = dot(second, q).reshape(part // group, group, EXTRA)
         side = side + pieces[None]
         send_ref[start : start + part, width:] = side.reshape(part, EXTRA).astype(BF16)
         out = pltpu.make_async_copy(
@@ -106,10 +108,12 @@
         out_shape=(
             jax.ShapeDtypeStruct((rows, width + EXTRA), BF16),
             jax.ShapeDtypeStruct((1, n_tok), jnp.int32),
+            jax.ShapeDtypeStruct((n_tok, experts), BF16),
         ),
         in_specs=[pl.BlockSpec(memory_space=pltpu.HBM)] * 5,
         out_specs=(
             pl.BlockSpec(memory_space=pltpu.HBM),
+            pl.BlockSpec(memory_space=pltpu.VMEM),
             pl.BlockSpec(memory_space=pltpu.VMEM),
         ),
         scratch_shapes=[
@@ -118,7 +122,6 @@
             pltpu.VMEM((2 * n_tok, width), BF16),
             pltpu.VMEM((n_tok, width), BF16),
             pltpu.VMEM((1, width), BF16),
-            pltpu.VMEM((n_tok, EXTRA), BF16),
             pltpu.VMEM((rows, width + EXTRA), BF16),
             pltpu.SemaphoreType.DMA((5,)),
             pltpu.SemaphoreType.DMA((PREP_PARTS,)),
@@ -148,7 +151,7 @@
 
 
 def expert_kernel(
-    recv_ref, w_in_ref, w_out_hbm, back_hbm,
+    recv_ref, w_in_ref, w_out_hbm, back_hbm, router_ref,
     w_out_ref, routed_ref, scaled_ref, side_ref, hgrad_ref, back_ref, part_ref, load_sems, sems,
 ):
     rows, width = scaled_ref.shape
@@ -170,14 +173,16 @@
         copy.start()
         stores.append(copy)
 
-    for k in range(0, width, EXTRA):
-        first, second = split_halves(recv_ref[:, k : k + EXTRA])
-        routed_ref[:, k : k + EXTRA] = first
-        scaled_ref[:, k : k + EXTRA] = second
+    for k in range(0, width, PIECE):
+        first, second = split_halves(recv_ref[:, k : k + PIECE])
+        routed_ref[:, k : k + PIECE] = first
+        scaled_ref[:, k : k + PIECE] = second
     pieces, q = split_halves(recv_ref[:, width:])
-    for i in range(EXTRA // 128):
-        side_ref[i] = pieces[:, i * 128 : (i + 1) * 128].astype(F32)
-    q = q[:, 0:experts].astype(F32)
+    side_ref[...] = pieces.astype(F32)
+    for k in range(CAP):
+        strip = side_ref[pl.ds(k, experts, stride=CAP), :]
+        router_ref[:, k * EXTRA : (k + 1) * EXTRA] = strip.astype(BF16)
+    q = q.astype(F32)
     c = jnp.zeros((rows, 128), F32)
     pre_all = dot(routed_ref[...], w_in_ref[0])
     for i in range(EXPERT_BLOCKS):
@@ -198,15 +203,12 @@
     store(half, 128)
 
     def grad_piece(k):
-        strips = [side_ref[i, pl.ds(k, experts, stride=CAP), :] for i in range(EXTRA // 128)]
-        router = jnp.concatenate(strips, axis=1).astype(BF16)
-        grad = dot(hgrad_ref[...], w_in_ref[0, k * EXTRA : (k + 1) * EXTRA, :], 1, 1)
-        return grad + dot(logit_grad, router)
-
-    for k in range(half // EXTRA):
-        joined = join_halves(grad_piece(k), grad_piece(half // EXTRA + k))
-        back_ref[:, k * EXTRA : (k + 1) * EXTRA] = joined.astype(BF16)
-        store(k * EXTRA, EXTRA)
+        return dot(hgrad_ref[...], w_in_ref[0, k * PIECE : (k + 1) * PIECE, :], 1, 1)
+
+    for k in range(half // PIECE):
+        joined = join_halves(grad_piece(k), grad_piece(half // PIECE + k))
+        back_ref[:, k * PIECE : (k + 1) * PIECE] = joined.astype(BF16)
+        store(k * PIECE, PIECE)
     for copy in stores:
         copy.wait()
 
@@ -219,23 +221,26 @@
     back_shape = (rows2, width // 2 + 128)
     return pl.pallas_call(
         expert_kernel,
-        out_shape=jax.ShapeDtypeStruct(back_shape, BF16),
+        out_shape=(
+            jax.ShapeDtypeStruct(back_shape, BF16),
+            jax.ShapeDtypeStruct((experts, CAP * EXTRA), BF16),
+        ),
         in_specs=[
             pl.BlockSpec(memory_space=pltpu.VMEM),
             pl.BlockSpec(memory_space=pltpu.VMEM),
             pl.BlockSpec(memory_space=pltpu.HBM),
         ],
-        out_specs=pl.BlockSpec(memory_space=pltpu.HBM),
+        out_specs=(pl.BlockSpec(memory_space=pltpu.HBM), pl.BlockSpec(memory_space=pltpu.VMEM)),
         scratch_shapes=[
             pltpu.VMEM((inner, width), BF16),
             pltpu.VMEM((rows, width), BF16),
             pltpu.VMEM((rows, width), BF16),
-            pltpu.VMEM((EXTRA // 128, rows, 128), F32),
+            pltpu.VMEM((rows, EXTRA), F32),
             pltpu.VMEM((rows, inner), BF16),
             pltpu.VMEM(back_shape, BF16),
             pltpu.VMEM((experts * 8, 128), F32),
             pltpu.SemaphoreType.DMA((EXPERT_BLOCKS,)),
-            pltpu.SemaphoreType.DMA((width // 2 // EXTRA + 1,)),
+            pltpu.SemaphoreType.DMA((width // 2 // PIECE + 1,)),
         ],
         compiler_params=pltpu.CompilerParams(vmem_limit_bytes=EXPERT_VMEM),
     )(recv, w_in, w_out)
@@ -246,10 +251,10 @@
 
     @pl.when(pl.program_id(0) == 0)
     def _():
-        for k in range(0, width, EXTRA):
-            first, second = split_halves(recv_ref[:, k : k + EXTRA])
-            routed_ref[:, k : k + EXTRA] = first
-            scaled_ref[:, k : k + EXTRA] = second
+        for k in range(0, width, PIECE):
+            first, second = split_halves(recv_ref[:, k : k + PIECE])
+            routed_ref[:, k : k + PIECE] = first
+            scaled_ref[:, k : k + PIECE] = second
 
     pre = dot(routed_ref[...], w_in_ref[0])
     back = dot(scaled_ref[...], w_out_ref[0], 1, 1)
@@ -286,7 +291,7 @@
     )(recv, w_in, w_out)
 
 
-def post_kernel(recv_ref, slot_ref, d_tok_ref, d_router_ref):
+def post_kernel(recv_ref, slot_ref, tok_ref, q_ref, own_ref, other_ref, odd_ref, d_tok_ref, d_router_ref):
     rows = recv_ref.shape[0]
     n_tok, width = d_tok_ref.shape
     half = width // 2
@@ -294,15 +299,24 @@
     slot = slot_ref[...]
     first = jnp.where(row == slot, 1.0, 0.0).astype(BF16)
     second = jnp.where(row == slot + CAP, 1.0, 0.0).astype(BF16)
-    d_tok_ref[:, 0:half] = dot(first, recv_ref[:, 0:half], 0, 0).astype(BF16)
-    d_tok_ref[:, half:] = dot(second, recv_ref[:, 0:half], 0, 0).astype(BF16)
+    left = dot(first, recv_ref[:, 0:half], 0, 0)
+    right = dot(second, recv_ref[:, 0:half], 0, 0)
+    product = tok_ref[:, 0:half].astype(F32) * left + tok_ref[:, half:].astype(F32) * right
+    c = jnp.sum(product, axis=1, keepdims=True)
+    logit_grad = (c * q_ref[...].astype(F32)).astype(BF16)
+    own = dot(logit_grad, own_ref[...])
+    other = dot(logit_grad, other_ref[...])
+    odd = odd_ref[...] > 0
+    d_tok_ref[:, 0:half] = (left + jnp.where(odd, other, own)).astype(BF16)
+    d_tok_ref[:, half:] = (right + jnp.where(odd, own, other)).astype(BF16)
     parts = recv_ref[:, half:].astype(F32).reshape(rows // 8, 8, 128)
     total = jnp.sum(parts, axis=0)
     for k in range(width // 128):
         d_router_ref[:, k * 128 : (k + 1) * 128] = total[k : k + 1, :]
 
 
-def post(recv, slot, n_tok, width):
+def post(recv, slot, tokens, q, own, other, odd):
+    n_tok, width = tokens.shape
     return pl.pallas_call(
         post_kernel,
         out_shape=(
@@ -310,7 +324,7 @@
             jax.ShapeDtypeStruct((1, width), F32),
         ),
         compiler_params=pltpu.CompilerParams(vmem_limit_bytes=POST_VMEM),
-    )(recv, slot)
+    )(recv, slot, tokens, q, own, other, odd)
 
 
 def exchange(rows, experts):
@@ -322,11 +336,17 @@
 def per_device(tokens, out_grad, expert_ids, router_logits, router_weight, w_in, w_out):
     experts = router_logits.shape[1]
     n_tok, width = tokens.shape
-    send, slot = prep(expert_ids.reshape(1, n_tok), router_logits, tokens, out_grad, router_weight)
+    send, slot, q = prep(
+        expert_ids.reshape(1, n_tok), router_logits, tokens, out_grad, router_weight
+    )
     recv = exchange(send, experts)
-    got = exchange(expert(recv, w_in, w_out), experts)
+    back, own = expert(recv, w_in, w_out)
+    got = exchange(back, experts)
+    swap = [(i, i ^ 1) for i in range(lax.axis_size("col"))]
+    other = lax.ppermute(own, "col", swap)
+    odd = jnp.full((1, 1), lax.axis_index("col") % 2, jnp.int32)
     d_in, d_out = weight_grads(recv, w_in, w_out)
-    d_tokens, d_router = post(got, slot, n_tok, width)
+    d_tokens, d_router = post(got, slot, tokens, q, own, other, odd)
     return (d_tokens, d_in, d_out, d_router)
 
 

time: 89.4 us -> 87.5 us (0.979)
  blocking collectives: 47.6 us -> 44.8 us
  starting transfers between devices: 4.42 us -> 5.86 us
  waiting for transfers between devices: 8.04 us -> 6.64 us
  local copies, waits for them, and re-layouts: 0.02 us -> 1.1 us
    all_to_all x1, blocking collectives: 47.6 us -> 44.8 us  [exchange(): lax.all_to_all(cut, AXES, split_axis=0, concat_axis=0, tiled=True)]
    ppermute x0 -> x1, starting transfers between devices: none -> 1.47 us  [per_device(): other = lax.ppermute(own, 'col', swap)]
    all_to_all x1, waiting for transfers between devices: 8.04 us -> 6.64 us  [exchange(): lax.all_to_all(cut, AXES, split_axis=0, concat_axis=0, tiled=True)]
    unnamed x6 -> x12, local copies, waits for them, and re-layouts: 0.02 us -> 1.1 us
  transfers between devices with their start and end apart: 1 -> 2, of which waited for: 1 -> 1; matrix products, arithmetic and copies ran while one was open for 0% -> 0% of each run, Pallas kernels for 15% -> 16%
where the time goes in v5:
time: 87.5 us; the launch traced here: 87.3 us
  blocking collectives  44.8 us (51%)
  Pallas kernels  28.1 us (32%)
  waiting for transfers between devices  6.64 us (8%)
  starting transfers between devices  5.86 us (7%)
  local copies, waits for them, and re-layouts  1.1 us (1%)
    all_to_all x1, blocking collectives, exchange(): lax.all_to_all(cut, AXES, split_axis=0, concat_axis=0, tiled=True)  44.8 us
    pallas_call x1, Pallas kernels, weight_grads(): pl.pallas_call(weight_kernel, grid=(BLOCKS,), out_shape=(jax.ShapeDtypeSt...  13.7 us
    pallas_call x1, Pallas kernels, expert(): pl.pallas_call(expert_kernel, out_shape=(jax.ShapeDtypeStruct(back_shape,...  8.4 us
    all_to_all x1, waiting for transfers between devices, exchange(): lax.all_to_all(cut, AXES, split_axis=0, concat_axis=0, tiled=True)  6.64 us
    all_to_all x1, starting transfers between devices, exchange(): lax.all_to_all(cut, AXES, split_axis=0, concat_axis=0, tiled=True)  4.4 us
    pallas_call x1, Pallas kernels, prep(): pl.pallas_call(prep_kernel, out_shape=(jax.ShapeDtypeStruct((rows, width...  4.18 us
    pallas_call x1, Pallas kernels, post(): pl.pallas_call(post_kernel, out_shape=(jax.ShapeDtypeStruct((n_tok, width...  1.9 us
  transfers between devices with their start and end apart: 2, of which 1 were waited for; matrix products, arithmetic and copies ran while one was open for 0% of the time, Pallas kernels for 16%

profile of v5, /device:TPU:1, one launch (start us, length us, event | category | flops | bytes accessed | tf_op | source)
XLA Modules:
  0.0 87.3 jit_solution(9301100673279058139)
XLA Ops:
  0.6 4.2 %shard_map.102 = (bf16[1024,1152]{1,0:T(8,128)(2,1)}, s32[1,256]{1,0:T(1,128)}, bf16[256,128]{1,0:T(8,128)(2,1)}) custom-call(s32[1,256]{1,0:T(1,128)} %bitcast.11, f32[256,128]{1,0:T(8,128)} %logits_hbm.1, bf16[256,1024]{1,0:T(8,128)(2,1)} %tok_ref.1, bf16[256,1024]{1,0:T(8,128)(2,1)} %og_hbm.1, bf16[1,1024]{1,0:T(2,128)(2,1)} %rw_hbm.1), custom_call_target="tpu_custom_call" | custom-call | tf_op jit(solution)/shard_map/pallas_call | solution.py:106
  4.8 0.0 copy-start.1
  4.8 44.8 %all_to_all.10 = bf16[128,8,1152]{2,1,0:T(8,128)(2,1)S(1)} all-to-all(bf16[128,8,1152]{2,1,0:T(8,128)(2,1)} %bitcast.10), channel_id=1, replica_groups=mesh['row'=4,'col'=32] {'row','col'}, dimensions={0} | all-to-all | bytes 4718592 | tf_op jit(solution)/shard_map/all_to_all | solution.py:333
  49.6 0.0 copy-start
  49.6 0.0 copy-done.1
  49.7 8.4 %shard_map.103 = (bf16[1024,640]{1,0:T(8,128)(2,1)S(1)}, bf16[128,512]{1,0:T(8,128)(2,1)S(1)}) custom-call(bf16[1024,1152]{1,0:T(8,128)(2,1)S(1)} %bitcast.6, bf16[1,1024,2048]{2,1,0:T(8,128)(2,1)S(1)} %copy-done.1, bf16[1,2048,1024]{2,1,0:T(8,128)(2,1)} %w_out_ref.1), custom_call_target="tpu_custom_call" | custom-call | tf_op jit(solution)/shard_map/pallas_call | solution.py:222
  58.1 0.0 copy-done
  58.1 0.0 copy-start.3
  58.1 1.1 %copy-done.3 = bf16[1024,640]{1,0:T(8,128)(2,1)} copy-done((bf16[1024,640]{1,0:T(8,128)(2,1)}, bf16[1024,640]{1,0:T(8,128)(2,1)S(1)}, u32[]{:S(2)}) %copy-start.3) | copy-done | bytes 1310744
  59.2 4.4 %all-to-all-start.1 = ((bf16[128,8,640]{2,1,0:T(8,128)(2,1)}), bf16[128,8,640]{2,1,0:T(8,128)(2,1)S(1)}, u32[]{:S(2)}, u32[]{:S(2)}) async-start(bf16[128,8,640]{2,1,0:T(8,128)(2,1)} %bitcast.9), calls=%async_computation.1 | async-start | bytes 2621440 | tf_op jit(solution)/shard_map/all_to_all | solution.py:333
  63.6 0.0 copy-start.2
  63.6 0.0 copy-start.4
  63.6 0.0 copy-start.5
  63.6 1.5 %collective-permute-start = (bf16[128,512]{1,0:T(8,128)(2,1)S(1)}, bf16[128,512]{1,0:T(8,128)(2,1)S(1)}, u32[]{:S(2)}, u32[]{:S(2)}) collective-permute-start(bf16[128,512]{1,0:T(8,128)(2,1)S(1)} %get-tuple-element.17.own_ref), channel_id=1, source_target_pairs={{0,1},{1,0},{2,3},{3,2},{4,5},{5,4},{6,7},{7,6},{8,9},{9,8},{10,11... | collective-permute-start | bytes 393224 | tf_op jit(solution)/shard_map/ppermute | solution.py:346
  65.1 13.7 %shard_map.105 = (bf16[1,1024,2048]{2,1,0:T(8,128)(2,1)}, bf16[1,2048,1024]{2,1,0:T(8,128)(2,1)}) custom-call(bf16[1024,1152]{1,0:T(8,128)(2,1)} %bitcast.7, bf16[1,1024,2048]{2,1,0:T(8,128)(2,1)} %w_in_ref.3, bf16[1,2048,1024]{2,1,0:T(8,128)(2,1)} %w_out_ref.1), custom_call_target="tpu_custom_call" | custom-call | flops 8589934592 | bytes 19136512 | tf_op jit(solution)/shard_map/pallas_call | solution.py:276
  78.7 0.0 collective-permute-done.other_ref
  78.7 6.6 %all-to-all-done.1 = bf16[128,8,640]{2,1,0:T(8,128)(2,1)S(1)} async-done(((bf16[128,8,640]{2,1,0:T(8,128)(2,1)}), bf16[128,8,640]{2,1,0:T(8,128)(2,1)S(1)}, u32[]{:S(2)}, u32[]{:S(2)}) %all-to-all-start.1) | async-done | bytes 1310752 | tf_op jit(solution)/shard_map/all_to_all | solution.py:333
  85.4 0.0 copy-done.2
  85.4 0.0 copy-done.4
  85.4 0.0 copy-done.5
  85.4 1.9 %shard_map.104 = (bf16[256,1024]{1,0:T(8,128)(2,1)}, f32[1,1024]{1,0:T(1,128)}) custom-call(bf16[1024,640]{1,0:T(8,128)(2,1)S(1)} %bitcast.8, s32[1,256]{1,0:T(1,128)S(1)} %copy-done.5, bf16[256,1024]{1,0:T(8,128)(2,1)S(1)} %copy-done.2, bf16[256,128]{1,0:T(8,128)(2,1)S(1)} %copy-done.4, bf16[128,512]{1,0:T(8,128)(2,1)S(1)} %get-tuple-element.17.own_ref, ...), custom_call_target="tpu_custom_call" | custom-call | tf_op jit(solution)/shard_map/pallas_call | solution.py:320
Async XLA Ops:
  4.8 44.8 %copy-start.1 = (bf16[1,1024,2048]{2,1,0:T(8,128)(2,1)S(1)}, bf16[1,1024,2048]{2,1,0:T(8,128)(2,1)}, u32[]{:S(2)}) copy-start(bf16[1,1024,2048]{2,1,0:T(8,128)(2,1)} %w_in_ref.3) | copy-start | bytes 12582916
  49.6 8.4 %copy-start = (bf16[128,8,1152]{2,1,0:T(8,128)(2,1)}, bf16[128,8,1152]{2,1,0:T(8,128)(2,1)S(1)}, u32[]{:S(2)}) copy-start(bf16[128,8,1152]{2,1,0:T(8,128)(2,1)S(1)} %all_to_all.10) | copy-start | bytes 7077892
  58.1 1.1 %copy-start.3 = (bf16[1024,640]{1,0:T(8,128)(2,1)}, bf16[1024,640]{1,0:T(8,128)(2,1)S(1)}, u32[]{:S(2)}) copy-start(bf16[1024,640]{1,0:T(8,128)(2,1)S(1)} %get-tuple-element.14) | copy-start | bytes 3932164
  59.2 26.2 %all-to-all-start.1 = ((bf16[128,8,640]{2,1,0:T(8,128)(2,1)}), bf16[128,8,640]{2,1,0:T(8,128)(2,1)S(1)}, u32[]{:S(2)}, u32[]{:S(2)}) async-start(bf16[128,8,640]{2,1,0:T(8,128)(2,1)} %bitcast.9), calls=%async_computation.1 | async-start | bytes 2621440 | tf_op jit(solution)/shard_map/all_to_all | solution.py:333
  63.6 21.8 %copy-start.2 = (bf16[256,1024]{1,0:T(8,128)(2,1)S(1)}, bf16[256,1024]{1,0:T(8,128)(2,1)}, u32[]{:S(2)}) copy-start(bf16[256,1024]{1,0:T(8,128)(2,1)} %tok_ref.1) | copy-start | bytes 1572868
  63.6 21.8 %copy-start.4 = (bf16[256,128]{1,0:T(8,128)(2,1)S(1)}, bf16[256,128]{1,0:T(8,128)(2,1)}, u32[]{:S(2)}) copy-start(bf16[256,128]{1,0:T(8,128)(2,1)} %get-tuple-element.16.q_ref) | copy-start | bytes 196612
  63.6 21.8 %copy-start.5 = (s32[1,256]{1,0:T(1,128)S(1)}, s32[1,256]{1,0:T(1,128)}, u32[]{:S(2)}) copy-start(s32[1,256]{1,0:T(1,128)} %get-tuple-element.15.slot_ref) | copy-start | bytes 3076
  63.6 15.1 %collective-permute-start = (bf16[128,512]{1,0:T(8,128)(2,1)S(1)}, bf16[128,512]{1,0:T(8,128)(2,1)S(1)}, u32[]{:S(2)}, u32[]{:S(2)}) collective-permute-start(bf16[128,512]{1,0:T(8,128)(2,1)S(1)} %get-tuple-element.17.own_ref), channel_id=1, source_target_pairs={{0,1},{1,0},{2,3},{3,2},{4,5},{5,4},{6,7},{7,6},{8,9},{9,8},{10,11... | collective-permute-start | bytes 393224 | tf_op jit(solution)/shard_map/ppermute | solution.py:346

commit v6 on v5

--- a/solution.py
+++ b/solution.py
@@ -151,8 +151,8 @@
 
 
 def expert_kernel(
-    recv_ref, w_in_ref, w_out_hbm, back_hbm, router_ref,
-    w_out_ref, routed_ref, scaled_ref, side_ref, hgrad_ref, back_ref, part_ref, load_sems, sems,
+    recv_ref, w_in_ref, w_out_hbm, back_ref, router_ref,
+    w_out_ref, routed_ref, scaled_ref, side_ref, hgrad_ref, part_ref, load_sems,
 ):
     rows, width = scaled_ref.shape
     inner = hgrad_ref.shape[1]
@@ -165,14 +165,6 @@
         load = pltpu.make_async_copy(w_out_hbm.at[0, cut, :], w_out_ref.at[cut, :], load_sems.at[i])
         load.start()
         loads.append(load)
-    stores = []
-
-    def store(start, size):
-        cut = pl.ds(start, size)
-        copy = pltpu.make_async_copy(back_ref.at[:, cut], back_hbm.at[:, cut], sems.at[len(stores)])
-        copy.start()
-        stores.append(copy)
-
     for k in range(0, width, PIECE):
         first, second = split_halves(recv_ref[:, k : k + PIECE])
         routed_ref[:, k : k + PIECE] = first
@@ -196,21 +188,17 @@
         for j in range(0, block, 128):
             c = c + product[:, j : j + 128]
     logit_grad = (jnp.sum(c, axis=1, keepdims=True) * q).astype(BF16)
+
+    def grad_piece(k):
+        return dot(hgrad_ref[...], w_in_ref[0, k * PIECE : (k + 1) * PIECE, :], 1, 1)
+
+    for k in range(half // PIECE):
+        joined = join_halves(grad_piece(k), grad_piece(half // PIECE + k))
+        back_ref[:, k * PIECE : (k + 1) * PIECE] = joined.astype(BF16)
     part = dot(logit_grad, routed_ref[...], 0, 0)
     for k in range(width // 128):
         part_ref[pl.ds(k, experts, stride=8), :] = part[:, k * 128 : (k + 1) * 128]
     back_ref[:, half:] = part_ref[...].astype(BF16)
-    store(half, 128)
-
-    def grad_piece(k):
-        return dot(hgrad_ref[...], w_in_ref[0, k * PIECE : (k + 1) * PIECE, :], 1, 1)
-
-    for k in range(half // PIECE):
-        joined = join_halves(grad_piece(k), grad_piece(half // PIECE + k))
-        back_ref[:, k * PIECE : (k + 1) * PIECE] = joined.astype(BF16)
-        store(k * PIECE, PIECE)
-    for copy in stores:
-        copy.wait()
 
 
 def expert(recv, w_in, w_out):
@@ -230,17 +218,15 @@
             pl.BlockSpec(memory_space=pltpu.VMEM),
             pl.BlockSpec(memory_space=pltpu.HBM),
         ],
-        out_specs=(pl.BlockSpec(memory_space=pltpu.HBM), pl.BlockSpec(memory_space=pltpu.VMEM)),
+        out_specs=(pl.BlockSpec(memory_space=pltpu.VMEM),) * 2,
         scratch_shapes=[
             pltpu.VMEM((inner, width), BF16),
             pltpu.VMEM((rows, width), BF16),
             pltpu.VMEM((rows, width), BF16),
             pltpu.VMEM((rows, EXTRA), F32),
             pltpu.VMEM((rows, inner), BF16),
-            pltpu.VMEM(back_shape, BF16),
             pltpu.VMEM((experts * 8, 128), F32),
             pltpu.SemaphoreType.DMA((EXPERT_BLOCKS,)),
-            pltpu.SemaphoreType.DMA((width // 2 // PIECE + 1,)),
         ],
         compiler_params=pltpu.CompilerParams(vmem_limit_bytes=EXPERT_VMEM),
     )(recv, w_in, w_out)

time: 87.5 us -> 86.7 us (level)
  no operation moved by 1% of the time
where the time goes in v6:
time: 86.7 us; the launch traced here: 86.5 us
  blocking collectives  44.8 us (52%)
  Pallas kernels  27.4 us (32%)
  waiting for transfers between devices  6.64 us (8%)
  starting transfers between devices  5.86 us (7%)
  local copies, waits for them, and re-layouts  1.1 us (1%)
    all_to_all x1, blocking collectives, exchange(): lax.all_to_all(cut, AXES, split_axis=0, concat_axis=0, tiled=True)  44.8 us
    pallas_call x1, Pallas kernels, weight_grads(): pl.pallas_call(weight_kernel, grid=(BLOCKS,), out_shape=(jax.ShapeDtypeSt...  13.7 us
    pallas_call x1, Pallas kernels, expert(): pl.pallas_call(expert_kernel, out_shape=(jax.ShapeDtypeStruct(back_shape,...  7.64 us
    all_to_all x1, waiting for transfers between devices, exchange(): lax.all_to_all(cut, AXES, split_axis=0, concat_axis=0, tiled=True)  6.64 us
    all_to_all x1, starting transfers between devices, exchange(): lax.all_to_all(cut, AXES, split_axis=0, concat_axis=0, tiled=True)  4.4 us
    pallas_call x1, Pallas kernels, prep(): pl.pallas_call(prep_kernel, out_shape=(jax.ShapeDtypeStruct((rows, width...  4.18 us
    pallas_call x1, Pallas kernels, post(): pl.pallas_call(post_kernel, out_shape=(jax.ShapeDtypeStruct((n_tok, width...  1.91 us
  transfers between devices with their start and end apart: 2, of which 1 were waited for; matrix products, arithmetic and copies ran while one was open for 0% of the time, Pallas kernels for 16%

profile of v6, /device:TPU:1, one launch (start us, length us, event | category | flops | bytes accessed | tf_op | source)
XLA Modules:
  0.0 86.5 jit_solution(2626244148036993782)
XLA Ops:
  0.6 4.2 %shard_map.102 = (bf16[1024,1152]{1,0:T(8,128)(2,1)}, s32[1,256]{1,0:T(1,128)}, bf16[256,128]{1,0:T(8,128)(2,1)}) custom-call(s32[1,256]{1,0:T(1,128)} %bitcast.11, f32[256,128]{1,0:T(8,128)} %logits_hbm.1, bf16[256,1024]{1,0:T(8,128)(2,1)} %tok_ref.1, bf16[256,1024]{1,0:T(8,128)(2,1)} %og_hbm.1, bf16[1,1024]{1,0:T(2,128)(2,1)} %rw_hbm.1), custom_call_target="tpu_custom_call" | custom-call | tf_op jit(solution)/shard_map/pallas_call | solution.py:106
  4.8 0.0 copy-start.1
  4.8 44.8 %all_to_all.10 = bf16[128,8,1152]{2,1,0:T(8,128)(2,1)S(1)} all-to-all(bf16[128,8,1152]{2,1,0:T(8,128)(2,1)} %bitcast.10), channel_id=1, replica_groups=mesh['row'=4,'col'=32] {'row','col'}, dimensions={0} | all-to-all | bytes 4718592 | tf_op jit(solution)/shard_map/all_to_all | solution.py:319
  49.6 0.0 copy-start
  49.6 0.0 copy-done.1
  49.7 7.6 %shard_map.103 = (bf16[1024,640]{1,0:T(8,128)(2,1)S(1)}, bf16[128,512]{1,0:T(8,128)(2,1)S(1)}) custom-call(bf16[1024,1152]{1,0:T(8,128)(2,1)S(1)} %bitcast.6, bf16[1,1024,2048]{2,1,0:T(8,128)(2,1)S(1)} %copy-done.1, bf16[1,2048,1024]{2,1,0:T(8,128)(2,1)} %w_out_ref.1), custom_call_target="tpu_custom_call" | custom-call | tf_op jit(solution)/shard_map/pallas_call | solution.py:210
  57.3 0.0 copy-done
  57.3 0.0 copy-start.3
  57.3 1.1 %copy-done.3 = bf16[1024,640]{1,0:T(8,128)(2,1)} copy-done((bf16[1024,640]{1,0:T(8,128)(2,1)}, bf16[1024,640]{1,0:T(8,128)(2,1)S(1)}, u32[]{:S(2)}) %copy-start.3) | copy-done | bytes 1310744
  58.4 4.4 %all-to-all-start.1 = ((bf16[128,8,640]{2,1,0:T(8,128)(2,1)}), bf16[128,8,640]{2,1,0:T(8,128)(2,1)S(1)}, u32[]{:S(2)}, u32[]{:S(2)}) async-start(bf16[128,8,640]{2,1,0:T(8,128)(2,1)} %bitcast.9), calls=%async_computation.1 | async-start | bytes 2621440 | tf_op jit(solution)/shard_map/all_to_all | solution.py:319
  62.8 0.0 copy-start.2
  62.8 0.0 copy-start.4
  62.8 0.0 copy-start.5
  62.8 1.5 %collective-permute-start = (bf16[128,512]{1,0:T(8,128)(2,1)S(1)}, bf16[128,512]{1,0:T(8,128)(2,1)S(1)}, u32[]{:S(2)}, u32[]{:S(2)}) collective-permute-start(bf16[128,512]{1,0:T(8,128)(2,1)S(1)} %get-tuple-element.17.own_ref), channel_id=1, source_target_pairs={{0,1},{1,0},{2,3},{3,2},{4,5},{5,4},{6,7},{7,6},{8,9},{9,8},{10,11... | collective-permute-start | bytes 393224 | tf_op jit(solution)/shard_map/ppermute | solution.py:332
  64.3 13.7 %shard_map.105 = (bf16[1,1024,2048]{2,1,0:T(8,128)(2,1)}, bf16[1,2048,1024]{2,1,0:T(8,128)(2,1)}) custom-call(bf16[1024,1152]{1,0:T(8,128)(2,1)} %bitcast.7, bf16[1,1024,2048]{2,1,0:T(8,128)(2,1)} %w_in_ref.3, bf16[1,2048,1024]{2,1,0:T(8,128)(2,1)} %w_out_ref.1), custom_call_target="tpu_custom_call" | custom-call | flops 8589934592 | bytes 19136512 | tf_op jit(solution)/shard_map/pallas_call | solution.py:262
  78.0 0.0 collective-permute-done.other_ref
  78.0 6.6 %all-to-all-done.1 = bf16[128,8,640]{2,1,0:T(8,128)(2,1)S(1)} async-done(((bf16[128,8,640]{2,1,0:T(8,128)(2,1)}), bf16[128,8,640]{2,1,0:T(8,128)(2,1)S(1)}, u32[]{:S(2)}, u32[]{:S(2)}) %all-to-all-start.1) | async-done | bytes 1310752 | tf_op jit(solution)/shard_map/all_to_all | solution.py:319
  84.6 0.0 copy-done.2
  84.6 0.0 copy-done.4
  84.6 0.0 copy-done.5
  84.6 1.9 %shard_map.104 = (bf16[256,1024]{1,0:T(8,128)(2,1)}, f32[1,1024]{1,0:T(1,128)}) custom-call(bf16[1024,640]{1,0:T(8,128)(2,1)S(1)} %bitcast.8, s32[1,256]{1,0:T(1,128)S(1)} %copy-done.5, bf16[256,1024]{1,0:T(8,128)(2,1)S(1)} %copy-done.2, bf16[256,128]{1,0:T(8,128)(2,1)S(1)} %copy-done.4, bf16[128,512]{1,0:T(8,128)(2,1)S(1)} %get-tuple-element.17.own_ref, ...), custom_call_target="tpu_custom_call" | custom-call | tf_op jit(solution)/shard_map/pallas_call | solution.py:306
Async XLA Ops:
  4.8 44.8 %copy-start.1 = (bf16[1,1024,2048]{2,1,0:T(8,128)(2,1)S(1)}, bf16[1,1024,2048]{2,1,0:T(8,128)(2,1)}, u32[]{:S(2)}) copy-start(bf16[1,1024,2048]{2,1,0:T(8,128)(2,1)} %w_in_ref.3) | copy-start | bytes 12582916
  49.6 7.7 %copy-start = (bf16[128,8,1152]{2,1,0:T(8,128)(2,1)}, bf16[128,8,1152]{2,1,0:T(8,128)(2,1)S(1)}, u32[]{:S(2)}) copy-start(bf16[128,8,1152]{2,1,0:T(8,128)(2,1)S(1)} %all_to_all.10) | copy-start | bytes 7077892
  57.3 1.1 %copy-start.3 = (bf16[1024,640]{1,0:T(8,128)(2,1)}, bf16[1024,640]{1,0:T(8,128)(2,1)S(1)}, u32[]{:S(2)}) copy-start(bf16[1024,640]{1,0:T(8,128)(2,1)S(1)} %get-tuple-element.14) | copy-start | bytes 3932164
  58.4 26.2 %all-to-all-start.1 = ((bf16[128,8,640]{2,1,0:T(8,128)(2,1)}), bf16[128,8,640]{2,1,0:T(8,128)(2,1)S(1)}, u32[]{:S(2)}, u32[]{:S(2)}) async-start(bf16[128,8,640]{2,1,0:T(8,128)(2,1)} %bitcast.9), calls=%async_computation.1 | async-start | bytes 2621440 | tf_op jit(solution)/shard_map/all_to_all | solution.py:319
  62.8 21.8 %copy-start.2 = (bf16[256,1024]{1,0:T(8,128)(2,1)S(1)}, bf16[256,1024]{1,0:T(8,128)(2,1)}, u32[]{:S(2)}) copy-start(bf16[256,1024]{1,0:T(8,128)(2,1)} %tok_ref.1) | copy-start | bytes 1572868
  62.8 21.8 %copy-start.4 = (bf16[256,128]{1,0:T(8,128)(2,1)S(1)}, bf16[256,128]{1,0:T(8,128)(2,1)}, u32[]{:S(2)}) copy-start(bf16[256,128]{1,0:T(8,128)(2,1)} %get-tuple-element.16.q_ref) | copy-start | bytes 196612
  62.8 21.8 %copy-start.5 = (s32[1,256]{1,0:T(1,128)S(1)}, s32[1,256]{1,0:T(1,128)}, u32[]{:S(2)}) copy-start(s32[1,256]{1,0:T(1,128)} %get-tuple-element.15.slot_ref) | copy-start | bytes 3076
  62.8 15.1 %collective-permute-start = (bf16[128,512]{1,0:T(8,128)(2,1)S(1)}, bf16[128,512]{1,0:T(8,128)(2,1)S(1)}, u32[]{:S(2)}, u32[]{:S(2)}) collective-permute-start(bf16[128,512]{1,0:T(8,128)(2,1)S(1)} %get-tuple-element.17.own_ref), channel_id=1, source_target_pairs={{0,1},{1,0},{2,3},{3,2},{4,5},{5,4},{6,7},{7,6},{8,9},{9,8},{10,11... | collective-permute-start | bytes 393224 | tf_op jit(solution)/shard_map/ppermute | solution.py:332

commit v7 on v6

--- a/solution.py
+++ b/solution.py
@@ -30,8 +30,8 @@
 
 
 def prep_kernel(
-    ids_hbm, logits_hbm, tok_hbm, og_hbm, rw_hbm, send_hbm, slot_ref, q_ref,
-    ids_ref, logits_ref, rhs_ref, og_ref, rw_ref, send_ref, sems, out_sems,
+    ids_hbm, logits_hbm, tok_hbm, og_hbm, rw_hbm, send_hbm, slot_hbm, q_hbm,
+    ids_ref, logits_ref, rhs_ref, og_ref, rw_ref, send_ref, slot_ref, q_ref, sems, out_sems,
 ):
     n_tok, width = og_ref.shape
     experts = logits_ref.shape[1]
@@ -58,6 +58,8 @@
     rank = jnp.sum(earlier * onehot_t, axis=0, keepdims=True)
     slot = ids * (2 * CAP) + rank.astype(jnp.int32)
     slot_ref[...] = slot
+    outs = [pltpu.make_async_copy(slot_ref, slot_hbm, out_sems.at[PREP_PARTS])]
+    outs[0].start()
     onehot = onehot_t.T
     copies[1].wait()
     logits = logits_ref[...]
@@ -66,6 +68,8 @@
     gate = jnp.sum(probs * onehot, axis=1, keepdims=True)
     q = (onehot - probs).astype(BF16)
     q_ref[...] = q
+    outs.append(pltpu.make_async_copy(q_ref, q_hbm, out_sems.at[PREP_PARTS + 1]))
+    outs[1].start()
     copies[2].wait()
     rhs_ref[pl.ds(n_tok, n_tok), :] = (gate * og_ref[...].astype(F32)).astype(BF16)
     copies[3].wait()
@@ -78,7 +82,6 @@
         piece = jnp.broadcast_to(router[:, k * EXTRA : (k + 1) * EXTRA], (group, EXTRA))
         pieces = jnp.where(place == k + k // CAP * CAP, piece, pieces)
     part = rows // PREP_PARTS
-    outs = []
     for start in range(0, rows, part):
         row = iota((part, n_tok), 0) + start
         first = jnp.where(row == slot, 1.0, 0.0).astype(BF16)
@@ -113,8 +116,8 @@
         in_specs=[pl.BlockSpec(memory_space=pltpu.HBM)] * 5,
         out_specs=(
             pl.BlockSpec(memory_space=pltpu.HBM),
-            pl.BlockSpec(memory_space=pltpu.VMEM),
-            pl.BlockSpec(memory_space=pltpu.VMEM),
+            pl.BlockSpec(memory_space=pltpu.HBM),
+            pl.BlockSpec(memory_space=pltpu.HBM),
         ),
         scratch_shapes=[
             pltpu.VMEM((1, n_tok), jnp.int32),
@@ -123,8 +126,10 @@
             pltpu.VMEM((n_tok, width), BF16),
             pltpu.VMEM((1, width), BF16),
             pltpu.VMEM((rows, width + EXTRA), BF16),
+            pltpu.VMEM((1, n_tok), jnp.int32),
+            pltpu.VMEM((n_tok, experts), BF16),
             pltpu.SemaphoreType.DMA((5,)),
-            pltpu.SemaphoreType.DMA((PREP_PARTS,)),
+            pltpu.SemaphoreType.DMA((PREP_PARTS + 2,)),
         ],
         compiler_params=pltpu.CompilerParams(vmem_limit_bytes=PREP_VMEM),
     )(ids, logits, tokens, out_grad, router_weight)

time: 86.7 us -> 86.1 us (level)
  no operation moved by 1% of the time
where the time goes in v7:
time: 86.1 us; the launch traced here: 85.9 us
  blocking collectives  44.8 us (52%)
  Pallas kernels  26.8 us (31%)
  waiting for transfers between devices  6.64 us (8%)
  starting transfers between devices  5.86 us (7%)
  local copies, waits for them, and re-layouts  1.1 us (1%)
    all_to_all x1, blocking collectives, exchange(): lax.all_to_all(cut, AXES, split_axis=0, concat_axis=0, tiled=True)  44.8 us
    pallas_call x1, Pallas kernels, weight_grads(): pl.pallas_call(weight_kernel, grid=(BLOCKS,), out_shape=(jax.ShapeDtypeSt...  13.7 us
    pallas_call x1, Pallas kernels, expert(): pl.pallas_call(expert_kernel, out_shape=(jax.ShapeDtypeStruct(back_shape,...  7.64 us
    all_to_all x1, waiting for transfers between devices, exchange(): lax.all_to_all(cut, AXES, split_axis=0, concat_axis=0, tiled=True)  6.64 us
    all_to_all x1, starting transfers between devices, exchange(): lax.all_to_all(cut, AXES, split_axis=0, concat_axis=0, tiled=True)  4.4 us
    pallas_call x1, Pallas kernels, prep(): pl.pallas_call(prep_kernel, out_shape=(jax.ShapeDtypeStruct((rows, width...  3.56 us
    pallas_call x1, Pallas kernels, post(): pl.pallas_call(post_kernel, out_shape=(jax.ShapeDtypeStruct((n_tok, width...  1.91 us
  transfers between devices with their start and end apart: 2, of which 1 were waited for; matrix products, arithmetic and copies ran while one was open for 0% of the time, Pallas kernels for 16%

profile of v7, /device:TPU:1, one launch (start us, length us, event | category | flops | bytes accessed | tf_op | source)
XLA Modules:
  0.0 85.9 jit_solution(5620724209300467082)
XLA Ops:
  0.6 3.6 %shard_map.102 = (bf16[1024,1152]{1,0:T(8,128)(2,1)}, s32[1,256]{1,0:T(1,128)}, bf16[256,128]{1,0:T(8,128)(2,1)}) custom-call(s32[1,256]{1,0:T(1,128)} %bitcast.11, f32[256,128]{1,0:T(8,128)} %logits_hbm.1, bf16[256,1024]{1,0:T(8,128)(2,1)} %tok_ref.1, bf16[256,1024]{1,0:T(8,128)(2,1)} %og_hbm.1, bf16[1,1024]{1,0:T(2,128)(2,1)} %rw_hbm.1), custom_call_target="tpu_custom_call" | custom-call | tf_op jit(solution)/shard_map/pallas_call | solution.py:109
  4.2 0.0 copy-start.1
  4.2 44.8 %all_to_all.10 = bf16[128,8,1152]{2,1,0:T(8,128)(2,1)S(1)} all-to-all(bf16[128,8,1152]{2,1,0:T(8,128)(2,1)} %bitcast.10), channel_id=1, replica_groups=mesh['row'=4,'col'=32] {'row','col'}, dimensions={0} | all-to-all | bytes 4718592 | tf_op jit(solution)/shard_map/all_to_all | solution.py:324
  49.0 0.0 copy-start
  49.0 0.0 copy-done.1
  49.0 7.6 %shard_map.103 = (bf16[1024,640]{1,0:T(8,128)(2,1)S(1)}, bf16[128,512]{1,0:T(8,128)(2,1)S(1)}) custom-call(bf16[1024,1152]{1,0:T(8,128)(2,1)S(1)} %bitcast.6, bf16[1,1024,2048]{2,1,0:T(8,128)(2,1)S(1)} %copy-done.1, bf16[1,2048,1024]{2,1,0:T(8,128)(2,1)} %w_out_ref.1), custom_call_target="tpu_custom_call" | custom-call | tf_op jit(solution)/shard_map/pallas_call | solution.py:215
  56.7 0.0 copy-done
  56.7 0.0 copy-start.3
  56.7 1.1 %copy-done.3 = bf16[1024,640]{1,0:T(8,128)(2,1)} copy-done((bf16[1024,640]{1,0:T(8,128)(2,1)}, bf16[1024,640]{1,0:T(8,128)(2,1)S(1)}, u32[]{:S(2)}) %copy-start.3) | copy-done | bytes 1310744
  57.8 4.4 %all-to-all-start.1 = ((bf16[128,8,640]{2,1,0:T(8,128)(2,1)}), bf16[128,8,640]{2,1,0:T(8,128)(2,1)S(1)}, u32[]{:S(2)}, u32[]{:S(2)}) async-start(bf16[128,8,640]{2,1,0:T(8,128)(2,1)} %bitcast.9), calls=%async_computation.1 | async-start | bytes 2621440 | tf_op jit(solution)/shard_map/all_to_all | solution.py:324
  62.2 0.0 copy-start.2
  62.2 0.0 copy-start.4
  62.2 0.0 copy-start.5
  62.2 1.5 %collective-permute-start = (bf16[128,512]{1,0:T(8,128)(2,1)S(1)}, bf16[128,512]{1,0:T(8,128)(2,1)S(1)}, u32[]{:S(2)}, u32[]{:S(2)}) collective-permute-start(bf16[128,512]{1,0:T(8,128)(2,1)S(1)} %get-tuple-element.17.own_ref), channel_id=1, source_target_pairs={{0,1},{1,0},{2,3},{3,2},{4,5},{5,4},{6,7},{7,6},{8,9},{9,8},{10,11... | collective-permute-start | bytes 393224 | tf_op jit(solution)/shard_map/ppermute | solution.py:337
  63.7 13.7 %shard_map.105 = (bf16[1,1024,2048]{2,1,0:T(8,128)(2,1)}, bf16[1,2048,1024]{2,1,0:T(8,128)(2,1)}) custom-call(bf16[1024,1152]{1,0:T(8,128)(2,1)} %bitcast.7, bf16[1,1024,2048]{2,1,0:T(8,128)(2,1)} %w_in_ref.3, bf16[1,2048,1024]{2,1,0:T(8,128)(2,1)} %w_out_ref.1), custom_call_target="tpu_custom_call" | custom-call | flops 8589934592 | bytes 19136512 | tf_op jit(solution)/shard_map/pallas_call | solution.py:267
  77.4 0.0 collective-permute-done.other_ref
  77.4 6.6 %all-to-all-done.1 = bf16[128,8,640]{2,1,0:T(8,128)(2,1)S(1)} async-done(((bf16[128,8,640]{2,1,0:T(8,128)(2,1)}), bf16[128,8,640]{2,1,0:T(8,128)(2,1)S(1)}, u32[]{:S(2)}, u32[]{:S(2)}) %all-to-all-start.1) | async-done | bytes 1310752 | tf_op jit(solution)/shard_map/all_to_all | solution.py:324
  84.0 0.0 copy-done.2
  84.0 0.0 copy-done.4
  84.0 0.0 copy-done.5
  84.0 1.9 %shard_map.104 = (bf16[256,1024]{1,0:T(8,128)(2,1)}, f32[1,1024]{1,0:T(1,128)}) custom-call(bf16[1024,640]{1,0:T(8,128)(2,1)S(1)} %bitcast.8, s32[1,256]{1,0:T(1,128)S(1)} %copy-done.5, bf16[256,1024]{1,0:T(8,128)(2,1)S(1)} %copy-done.2, bf16[256,128]{1,0:T(8,128)(2,1)S(1)} %copy-done.4, bf16[128,512]{1,0:T(8,128)(2,1)S(1)} %get-tuple-element.17.own_ref, ...), custom_call_target="tpu_custom_call" | custom-call | tf_op jit(solution)/shard_map/pallas_call | solution.py:311
Async XLA Ops:
  4.2 44.8 %copy-start.1 = (bf16[1,1024,2048]{2,1,0:T(8,128)(2,1)S(1)}, bf16[1,1024,2048]{2,1,0:T(8,128)(2,1)}, u32[]{:S(2)}) copy-start(bf16[1,1024,2048]{2,1,0:T(8,128)(2,1)} %w_in_ref.3) | copy-start | bytes 12582916
  49.0 7.7 %copy-start = (bf16[128,8,1152]{2,1,0:T(8,128)(2,1)}, bf16[128,8,1152]{2,1,0:T(8,128)(2,1)S(1)}, u32[]{:S(2)}) copy-start(bf16[128,8,1152]{2,1,0:T(8,128)(2,1)S(1)} %all_to_all.10) | copy-start | bytes 7077892
  56.7 1.1 %copy-start.3 = (bf16[1024,640]{1,0:T(8,128)(2,1)}, bf16[1024,640]{1,0:T(8,128)(2,1)S(1)}, u32[]{:S(2)}) copy-start(bf16[1024,640]{1,0:T(8,128)(2,1)S(1)} %get-tuple-element.14) | copy-start | bytes 3932164
  57.8 26.2 %all-to-all-start.1 = ((bf16[128,8,640]{2,1,0:T(8,128)(2,1)}), bf16[128,8,640]{2,1,0:T(8,128)(2,1)S(1)}, u32[]{:S(2)}, u32[]{:S(2)}) async-start(bf16[128,8,640]{2,1,0:T(8,128)(2,1)} %bitcast.9), calls=%async_computation.1 | async-start | bytes 2621440 | tf_op jit(solution)/shard_map/all_to_all | solution.py:324
  62.2 21.8 %copy-start.2 = (bf16[256,1024]{1,0:T(8,128)(2,1)S(1)}, bf16[256,1024]{1,0:T(8,128)(2,1)}, u32[]{:S(2)}) copy-start(bf16[256,1024]{1,0:T(8,128)(2,1)} %tok_ref.1) | copy-start | bytes 1572868
  62.2 21.8 %copy-start.4 = (bf16[256,128]{1,0:T(8,128)(2,1)S(1)}, bf16[256,128]{1,0:T(8,128)(2,1)}, u32[]{:S(2)}) copy-start(bf16[256,128]{1,0:T(8,128)(2,1)} %get-tuple-element.16.q_ref) | copy-start | bytes 196612
  62.2 21.8 %copy-start.5 = (s32[1,256]{1,0:T(1,128)S(1)}, s32[1,256]{1,0:T(1,128)}, u32[]{:S(2)}) copy-start(s32[1,256]{1,0:T(1,128)} %get-tuple-element.15.slot_ref) | copy-start | bytes 3076
  62.2 15.1 %collective-permute-start = (bf16[128,512]{1,0:T(8,128)(2,1)S(1)}, bf16[128,512]{1,0:T(8,128)(2,1)S(1)}, u32[]{:S(2)}, u32[]{:S(2)}) collective-permute-start(bf16[128,512]{1,0:T(8,128)(2,1)S(1)} %get-tuple-element.17.own_ref), channel_id=1, source_target_pairs={{0,1},{1,0},{2,3},{3,2},{4,5},{5,4},{6,7},{7,6},{8,9},{9,8},{10,11... | collective-permute-start | bytes 393224 | tf_op jit(solution)/shard_map/ppermute | solution.py:337

commit v8 on v7

--- a/solution.py
+++ b/solution.py
@@ -282,7 +282,7 @@
     )(recv, w_in, w_out)
 
 
-def post_kernel(recv_ref, slot_ref, tok_ref, q_ref, own_ref, other_ref, odd_ref, d_tok_ref, d_router_ref):
+def post_kernel(recv_ref, slot_ref, tok_ref, q_ref, own_ref, other_ref, odd_ref, d_tok_hbm, d_router_ref, d_tok_ref, sems):
     rows = recv_ref.shape[0]
     n_tok, width = d_tok_ref.shape
     half = width // 2
@@ -299,11 +299,19 @@
     other = dot(logit_grad, other_ref[...])
     odd = odd_ref[...] > 0
     d_tok_ref[:, 0:half] = (left + jnp.where(odd, other, own)).astype(BF16)
+    outs = [
+        pltpu.make_async_copy(d_tok_ref.at[:, cut], d_tok_hbm.at[:, cut], sems.at[i])
+        for i, cut in enumerate((pl.ds(0, half), pl.ds(half, half)))
+    ]
+    outs[0].start()
     d_tok_ref[:, half:] = (right + jnp.where(odd, own, other)).astype(BF16)
+    outs[1].start()
     parts = recv_ref[:, half:].astype(F32).reshape(rows // 8, 8, 128)
     total = jnp.sum(parts, axis=0)
     for k in range(width // 128):
         d_router_ref[:, k * 128 : (k + 1) * 128] = total[k : k + 1, :]
+    for out in outs:
+        out.wait()
 
 
 def post(recv, slot, tokens, q, own, other, odd):
@@ -314,6 +322,9 @@
             jax.ShapeDtypeStruct((n_tok, width), BF16),
             jax.ShapeDtypeStruct((1, width), F32),
         ),
+        in_specs=[pl.BlockSpec(memory_space=pltpu.VMEM)] * 7,
+        out_specs=(pl.BlockSpec(memory_space=pltpu.HBM), pl.BlockSpec(memory_space=pltpu.VMEM)),
+        scratch_shapes=[pltpu.VMEM((n_tok, width), BF16), pltpu.SemaphoreType.DMA((2,))],
         compiler_params=pltpu.CompilerParams(vmem_limit_bytes=POST_VMEM),
     )(recv, slot, tokens, q, own, other, odd)
 

time: 86.1 us -> 86.9 us (level)
  no operation moved by 1% of the time
where the time goes in v8:
time: 86.9 us; the launch traced here: 86.7 us
  blocking collectives  44.8 us (52%)
  Pallas kernels  27.3 us (31%)
  waiting for transfers between devices  6.64 us (8%)
  starting transfers between devices  5.86 us (7%)
  local copies, waits for them, and re-layouts  1.1 us (1%)
  between operations  0.88 us (1%)
    all_to_all x1, blocking collectives, exchange(): lax.all_to_all(cut, AXES, split_axis=0, concat_axis=0, tiled=True)  44.8 us
    pallas_call x1, Pallas kernels, weight_grads(): pl.pallas_call(weight_kernel, grid=(BLOCKS,), out_shape=(jax.ShapeDtypeSt...  13.7 us
    pallas_call x1, Pallas kernels, expert(): pl.pallas_call(expert_kernel, out_shape=(jax.ShapeDtypeStruct(back_shape,...  7.64 us
    all_to_all x1, waiting for transfers between devices, exchange(): lax.all_to_all(cut, AXES, split_axis=0, concat_axis=0, tiled=True)  6.64 us
    all_to_all x1, starting transfers between devices, exchange(): lax.all_to_all(cut, AXES, split_axis=0, concat_axis=0, tiled=True)  4.4 us
    pallas_call x1, Pallas kernels, prep(): pl.pallas_call(prep_kernel, out_shape=(jax.ShapeDtypeStruct((rows, width...  3.56 us
    pallas_call x1, Pallas kernels, post(): pl.pallas_call(post_kernel, out_shape=(jax.ShapeDtypeStruct((n_tok, width...  2.49 us
  transfers between devices with their start and end apart: 2, of which 1 were waited for; matrix products, arithmetic and copies ran while one was open for 0% of the time, Pallas kernels for 16%

profile of v8, /device:TPU:1, one launch (start us, length us, event | category | flops | bytes accessed | tf_op | source)
XLA Modules:
  0.0 86.7 jit_solution(11238544512260800939)
XLA Ops:
  0.6 3.6 %shard_map.102 = (bf16[1024,1152]{1,0:T(8,128)(2,1)}, s32[1,256]{1,0:T(1,128)}, bf16[256,128]{1,0:T(8,128)(2,1)}) custom-call(s32[1,256]{1,0:T(1,128)} %bitcast.11, f32[256,128]{1,0:T(8,128)} %logits_hbm.1, bf16[256,1024]{1,0:T(8,128)(2,1)} %tok_ref.1, bf16[256,1024]{1,0:T(8,128)(2,1)} %og_hbm.1, bf16[1,1024]{1,0:T(2,128)(2,1)} %rw_hbm.1), custom_call_target="tpu_custom_call" | custom-call | tf_op jit(solution)/shard_map/pallas_call | solution.py:109
  4.2 0.0 copy-start.1
  4.2 44.8 %all_to_all.10 = bf16[128,8,1152]{2,1,0:T(8,128)(2,1)S(1)} all-to-all(bf16[128,8,1152]{2,1,0:T(8,128)(2,1)} %bitcast.10), channel_id=1, replica_groups=mesh['row'=4,'col'=32] {'row','col'}, dimensions={0} | all-to-all | bytes 4718592 | tf_op jit(solution)/shard_map/all_to_all | solution.py:335
  49.0 0.0 copy-start
  49.0 0.0 copy-done.1
  49.0 7.6 %shard_map.103 = (bf16[1024,640]{1,0:T(8,128)(2,1)S(1)}, bf16[128,512]{1,0:T(8,128)(2,1)S(1)}) custom-call(bf16[1024,1152]{1,0:T(8,128)(2,1)S(1)} %bitcast.6, bf16[1,1024,2048]{2,1,0:T(8,128)(2,1)S(1)} %copy-done.1, bf16[1,2048,1024]{2,1,0:T(8,128)(2,1)} %w_out_ref.1), custom_call_target="tpu_custom_call" | custom-call | tf_op jit(solution)/shard_map/pallas_call | solution.py:215
  56.7 0.0 copy-done
  56.7 0.0 copy-start.3
  56.7 1.1 %copy-done.3 = bf16[1024,640]{1,0:T(8,128)(2,1)} copy-done((bf16[1024,640]{1,0:T(8,128)(2,1)}, bf16[1024,640]{1,0:T(8,128)(2,1)S(1)}, u32[]{:S(2)}) %copy-start.3) | copy-done | bytes 1310744
  57.8 4.4 %all-to-all-start.1 = ((bf16[128,8,640]{2,1,0:T(8,128)(2,1)}), bf16[128,8,640]{2,1,0:T(8,128)(2,1)S(1)}, u32[]{:S(2)}, u32[]{:S(2)}) async-start(bf16[128,8,640]{2,1,0:T(8,128)(2,1)} %bitcast.9), calls=%async_computation.1 | async-start | bytes 2621440 | tf_op jit(solution)/shard_map/all_to_all | solution.py:335
  62.2 0.0 copy-start.2
  62.2 0.0 copy-start.4
  62.2 0.0 copy-start.5
  62.2 1.5 %collective-permute-start = (bf16[128,512]{1,0:T(8,128)(2,1)S(1)}, bf16[128,512]{1,0:T(8,128)(2,1)S(1)}, u32[]{:S(2)}, u32[]{:S(2)}) collective-permute-start(bf16[128,512]{1,0:T(8,128)(2,1)S(1)} %get-tuple-element.17.own_ref), channel_id=1, source_target_pairs={{0,1},{1,0},{2,3},{3,2},{4,5},{5,4},{6,7},{7,6},{8,9},{9,8},{10,11... | collective-permute-start | bytes 393224 | tf_op jit(solution)/shard_map/ppermute | solution.py:348
  63.7 13.7 %shard_map.105 = (bf16[1,1024,2048]{2,1,0:T(8,128)(2,1)}, bf16[1,2048,1024]{2,1,0:T(8,128)(2,1)}) custom-call(bf16[1024,1152]{1,0:T(8,128)(2,1)} %bitcast.7, bf16[1,1024,2048]{2,1,0:T(8,128)(2,1)} %w_in_ref.3, bf16[1,2048,1024]{2,1,0:T(8,128)(2,1)} %w_out_ref.1), custom_call_target="tpu_custom_call" | custom-call | flops 8589934592 | bytes 19136512 | tf_op jit(solution)/shard_map/pallas_call | solution.py:267
  77.4 0.0 collective-permute-done.other_ref
  77.4 6.6 %all-to-all-done.1 = bf16[128,8,640]{2,1,0:T(8,128)(2,1)S(1)} async-done(((bf16[128,8,640]{2,1,0:T(8,128)(2,1)}), bf16[128,8,640]{2,1,0:T(8,128)(2,1)S(1)}, u32[]{:S(2)}, u32[]{:S(2)}) %all-to-all-start.1) | async-done | bytes 1310752 | tf_op jit(solution)/shard_map/all_to_all | solution.py:335
  84.0 0.0 copy-done.2
  84.0 0.0 copy-done.4
  84.0 0.0 copy-done.5
  84.0 2.5 %shard_map.104 = (bf16[256,1024]{1,0:T(8,128)(2,1)}, f32[1,1024]{1,0:T(1,128)}) custom-call(bf16[1024,640]{1,0:T(8,128)(2,1)S(1)} %bitcast.8, s32[1,256]{1,0:T(1,128)S(1)} %copy-done.5, bf16[256,1024]{1,0:T(8,128)(2,1)S(1)} %copy-done.2, bf16[256,128]{1,0:T(8,128)(2,1)S(1)} %copy-done.4, bf16[128,512]{1,0:T(8,128)(2,1)S(1)} %get-tuple-element.17.own_ref, ...), custom_call_target="tpu_custom_call" | custom-call | tf_op jit(solution)/shard_map/pallas_call | solution.py:319
Async XLA Ops:
  4.2 44.8 %copy-start.1 = (bf16[1,1024,2048]{2,1,0:T(8,128)(2,1)S(1)}, bf16[1,1024,2048]{2,1,0:T(8,128)(2,1)}, u32[]{:S(2)}) copy-start(bf16[1,1024,2048]{2,1,0:T(8,128)(2,1)} %w_in_ref.3) | copy-start | bytes 12582916
  49.0 7.7 %copy-start = (bf16[128,8,1152]{2,1,0:T(8,128)(2,1)}, bf16[128,8,1152]{2,1,0:T(8,128)(2,1)S(1)}, u32[]{:S(2)}) copy-start(bf16[128,8,1152]{2,1,0:T(8,128)(2,1)S(1)} %all_to_all.10) | copy-start | bytes 7077892
  56.7 1.1 %copy-start.3 = (bf16[1024,640]{1,0:T(8,128)(2,1)}, bf16[1024,640]{1,0:T(8,128)(2,1)S(1)}, u32[]{:S(2)}) copy-start(bf16[1024,640]{1,0:T(8,128)(2,1)S(1)} %get-tuple-element.14) | copy-start | bytes 3932164
  57.8 26.2 %all-to-all-start.1 = ((bf16[128,8,640]{2,1,0:T(8,128)(2,1)}), bf16[128,8,640]{2,1,0:T(8,128)(2,1)S(1)}, u32[]{:S(2)}, u32[]{:S(2)}) async-start(bf16[128,8,640]{2,1,0:T(8,128)(2,1)} %bitcast.9), calls=%async_computation.1 | async-start | bytes 2621440 | tf_op jit(solution)/shard_map/all_to_all | solution.py:335
  62.2 21.8 %copy-start.2 = (bf16[256,1024]{1,0:T(8,128)(2,1)S(1)}, bf16[256,1024]{1,0:T(8,128)(2,1)}, u32[]{:S(2)}) copy-start(bf16[256,1024]{1,0:T(8,128)(2,1)} %tok_ref.1) | copy-start | bytes 1572868
  62.2 21.8 %copy-start.4 = (bf16[256,128]{1,0:T(8,128)(2,1)S(1)}, bf16[256,128]{1,0:T(8,128)(2,1)}, u32[]{:S(2)}) copy-start(bf16[256,128]{1,0:T(8,128)(2,1)} %get-tuple-element.16.q_ref) | copy-start | bytes 196612
  62.2 21.8 %copy-start.5 = (s32[1,256]{1,0:T(1,128)S(1)}, s32[1,256]{1,0:T(1,128)}, u32[]{:S(2)}) copy-start(s32[1,256]{1,0:T(1,128)} %get-tuple-element.15.slot_ref) | copy-start | bytes 3076
  62.2 15.1 %collective-permute-start = (bf16[128,512]{1,0:T(8,128)(2,1)S(1)}, bf16[128,512]{1,0:T(8,128)(2,1)S(1)}, u32[]{:S(2)}, u32[]{:S(2)}) collective-permute-start(bf16[128,512]{1,0:T(8,128)(2,1)S(1)} %get-tuple-element.17.own_ref), channel_id=1, source_target_pairs={{0,1},{1,0},{2,3},{3,2},{4,5},{5,4},{6,7},{7,6},{8,9},{9,8},{10,11... | collective-permute-start | bytes 393224 | tf_op jit(solution)/shard_map/ppermute | solution.py:348
